TPU v7x, 128 devices: a whole 4x4x4 slice. The times are simulated.
128 devices in a mesh: gx: 16 (over y, x), gy: 8 (over z, core).
Axes of the slice: x: 4, y: 4, z: 4, core: 2. Of those that a mesh axis runs over, the one named last changes fastest.
Arguments:
- coefficient: float32 [2, 2, 2, 128, 128, 128], P(None, None, None, 'gx', 'gy'), may hold values from 0.05 to 5
- owner: int32 [128, 128], P('gx', 'gy'), may hold values from 0 to 127, as said below
- w_in: bfloat16 [128, 27], replicated, may hold values from -1.25 to 1.25
- b_in: float32 [128], replicated, may hold values from -3 to 3
- w_mid: bfloat16 [2, 128, 128], replicated, may hold values from -0.5 to 0.5
- b_mid: float32 [2, 128], replicated, may hold values from -3 to 3
- w_out: bfloat16 [27, 128], replicated, may hold values from -0.5 to 0.5
- b_out: float32 [27], replicated, may hold values from -4 to 4
Outputs:
- relaid: float32 [32768, 27, 128], P(('gx', 'gy'))
Inputs may be any that keep to these rules, and one draw needn't show every extreme that they name: Among the 8 x 16 columns of one device, no owner appears more than 2 times, and one owner, the same for every device, appears exactly 2 times on every device.
All inputs are finite; a program needn't handle non-finite values.
Results may differ from a plain program's by a relative error of at most 0.004.
Values sent between devices are 32-bit elements; how exact they have to be, the bound alone decides.
No kernel may reach another device: no remote copies, remote signals or barrier semaphores. Data moves between devices by JAX's collectives and lax.ppermute only.
A program may use at most 128 MiB of HBM per device.

v0:
```python
import jax
import jax.numpy as jnp
from jax import lax
from jax.sharding import PartitionSpec as P


def extended(x, sides, width):
    for axis, dim in sides:
        size, length = (lax.axis_size(axis), x.shape[dim])
        up = [(i, (i + 1) % size) for i in range(size - 1)]
        down = [(j, i) for i, j in up]
        last = lax.slice_in_dim(x, length - width, length, axis=dim)
        first = lax.slice_in_dim(x, 0, width, axis=dim)
        before = lax.ppermute(last, axis, up)
        after = lax.ppermute(first, axis, down)
        x = jnp.concatenate([before, x, after], axis=dim)
    return x


def offset_list():
    return [
        (shift_x, shift_y, shift_z)
        for shift_x in (-1, 0, 1)
        for shift_y in (-1, 0, 1)
        for shift_z in (-1, 0, 1)
    ]


def parity_key(offset):
    return tuple((0 if component == 0 else 1 for component in offset))


def shift_next(values, which_axis):
    length = values.shape[which_axis]
    upper_part = lax.slice_in_dim(values, 1, length, axis=which_axis)
    filler = jnp.zeros_like(lax.slice_in_dim(values, 0, 1, axis=which_axis))
    return jnp.concatenate([upper_part, filler], axis=which_axis)


def shift_prev(values, which_axis):
    length = values.shape[which_axis]
    lower_part = lax.slice_in_dim(values, 0, length - 1, axis=which_axis)
    filler = jnp.zeros_like(lax.slice_in_dim(values, 0, 1, axis=which_axis))
    return jnp.concatenate([filler, lower_part], axis=which_axis)


def gather_offsets(fine_field):
    fields = []
    for offset in offset_list():
        portion = fine_field[parity_key(offset)]
        for which_axis, component in enumerate(offset):
            if component == -1:
                portion = shift_prev(portion, which_axis)
        fields.append(portion)
    return fields


def restrict(fine_field, weights):
    fields = gather_offsets(fine_field)
    accumulated = weights[0] * fields[0]
    for index_o in range(1, len(fields)):
        accumulated = accumulated + weights[index_o] * fields[index_o]
    return accumulated


def prolong(weights):
    parity_sums = {}
    for index_o, offset in enumerate(offset_list()):
        portion = weights[index_o]
        for which_axis, component in enumerate(offset):
            if component == -1:
                portion = shift_next(portion, which_axis)
        target = parity_key(offset)
        if target in parity_sums:
            parity_sums[target] = parity_sums[target] + portion
        else:
            parity_sums[target] = portion
    return jnp.stack(
        [
            jnp.stack(
                [
                    jnp.stack([parity_sums[parity_x, parity_y, parity_z] for parity_z in (0, 1)])
                    for parity_y in (0, 1)
                ]
            )
            for parity_x in (0, 1)
        ]
    )


def step_plus(values, which_axis):
    even_part = lax.slice_in_dim(values, 0, 1, axis=which_axis)
    odd_part = lax.slice_in_dim(values, 1, 2, axis=which_axis)
    return jnp.concatenate([odd_part, shift_next(even_part, which_axis + 3)], axis=which_axis)


def step_minus(values, which_axis):
    even_part = lax.slice_in_dim(values, 0, 1, axis=which_axis)
    odd_part = lax.slice_in_dim(values, 1, 2, axis=which_axis)
    return jnp.concatenate([shift_prev(odd_part, which_axis + 3), even_part], axis=which_axis)


def operate(field, face_coef):
    accumulated = jnp.zeros_like(field)
    for which_axis in range(3):
        face = face_coef[which_axis]
        accumulated = accumulated + face * (field - step_plus(field, which_axis))
        accumulated = accumulated + step_minus(face, which_axis) * (
            field - step_minus(field, which_axis)
        )
    return accumulated


def pick_offsets(probe_stack):
    for which_axis in range(3):
        grid_shape = [1] * probe_stack.ndim
        grid_shape[which_axis + 3] = probe_stack.shape[which_axis + 3]
        position = lax.broadcasted_iota(jnp.int32, tuple(grid_shape), which_axis + 3)
        picked_rows = []
        for offset in (-1, 0, 1):
            wanted = (position + offset + 3) % 3
            chosen = jnp.zeros_like(lax.slice_in_dim(probe_stack, 0, 1, axis=which_axis))
            for probe_class in range(3):
                chosen = chosen + jnp.where(
                    wanted == probe_class,
                    lax.slice_in_dim(probe_stack, probe_class, probe_class + 1, axis=which_axis),
                    0.0,
                )
            picked_rows.append(chosen)
        probe_stack = jnp.concatenate(picked_rows, axis=which_axis)
    return probe_stack


def galerkin(weights_ext, kappa_ext):
    face_coef = [jnp.sqrt(kappa_ext * step_plus(kappa_ext, which_axis)) for which_axis in range(3)]
    grid_shape = weights_ext.shape[1:]
    place_x = lax.broadcasted_iota(jnp.int32, grid_shape, 0) % 3
    place_y = lax.broadcasted_iota(jnp.int32, grid_shape, 1) % 3
    place_z = lax.broadcasted_iota(jnp.int32, grid_shape, 2) % 3

    def probe(probe_class, probe_stack):
        chosen = (
            (place_x == probe_class // 9)
            & (place_y == probe_class // 3 % 3)
            & (place_z == probe_class % 3)
        )
        masked = jnp.where(chosen[None], weights_ext, 0.0)
        applied = operate(prolong(masked), face_coef)
        return lax.dynamic_update_index_in_dim(
            probe_stack, restrict(applied, weights_ext), probe_class, 0
        )

    probe_stack = lax.fori_loop(0, 27, probe, jnp.zeros(weights_ext.shape, jnp.float32))
    picked = pick_offsets(probe_stack.reshape((3, 3, 3) + grid_shape)).reshape(weights_ext.shape)
    return picked[:, 1:-1, 1:-1, 1:-1]


def predict(feature_rows, w_in, b_in, w_mid, b_mid, w_out, b_out):
    hidden = jax.nn.silu(
        jnp.dot(w_in, feature_rows, preferred_element_type=jnp.float32) + b_in[:, None]
    ).astype(jnp.bfloat16)
    for layer_num in range(w_mid.shape[0]):
        hidden = jax.nn.silu(
            jnp.dot(w_mid[layer_num], hidden, preferred_element_type=jnp.float32)
            + b_mid[layer_num][:, None]
        ).astype(jnp.bfloat16)
    return 0.5 * jax.nn.sigmoid(
        jnp.dot(w_out, hidden, preferred_element_type=jnp.float32) + b_out[:, None]
    )


def coarse_features(kappa_ext):
    raw_features = jnp.stack(gather_offsets(jnp.log1p(kappa_ext)))[:, 1:-1, 1:-1, 1:-1]
    return raw_features.astype(jnp.bfloat16)


def per_device(coefficient, owner, w_in, b_in, w_mid, b_mid, w_out, b_out):
    z_padding = ((0, 0), (0, 0), (0, 0), (0, 0), (0, 0), (1, 1))
    kappa_ext = extended(coefficient, (("gx", 3), ("gy", 4)), 1)
    kappa_ext = jnp.pad(kappa_ext, z_padding)
    feature_grid = coarse_features(kappa_ext)
    weights = predict(
        feature_grid.reshape(feature_grid.shape[0], -1), w_in, b_in, w_mid, b_mid, w_out, b_out
    ).reshape(feature_grid.shape)
    weights_ext = extended(weights, (("gx", 1), ("gy", 2)), 1)
    weights_ext = jnp.pad(weights_ext, ((0, 0), (0, 0), (0, 0), (1, 1)))
    stencil = galerkin(weights_ext, kappa_ext)
    points = stencil.shape[0]
    depth = stencil.shape[3]
    columns = stencil.shape[1] * stencil.shape[2]
    devices = lax.axis_size("gx") * lax.axis_size("gy")
    per_pair = 2 * columns // devices
    blocks = jnp.transpose(stencil, (1, 2, 0, 3)).reshape(columns, points, depth)
    owners = owner.reshape(-1)
    matches = (owners[:, None] == jnp.arange(devices, dtype=jnp.int32)[None, :]).astype(jnp.int32)
    order_rank = jnp.sum(jnp.cumsum(matches, axis=0) * matches, axis=1) - 1
    slot_index = (owners * per_pair + order_rank).astype(jnp.int32)
    outgoing = (
        jnp.zeros((devices * per_pair, points, depth), jnp.float32).at[slot_index].set(blocks)
    )
    outgoing = outgoing.reshape(devices, per_pair, points, depth)
    incoming = lax.all_to_all(outgoing, ("gx", "gy"), split_axis=0, concat_axis=0, tiled=True)
    return incoming.reshape(devices * per_pair, points, depth)


def solution(mesh):
    return jax.shard_map(
        per_device,
        mesh=mesh,
        in_specs=(
            P(None, None, None, "gx", "gy", None),
            P("gx", "gy"),
            P(),
            P(),
            P(),
            P(),
            P(),
            P(),
        ),
        out_specs=P(("gx", "gy"), None, None),
        check_vma=False,
    )
```

profile of v0, /device:TPU:1, one launch (start us, length us, event | category | flops | bytes accessed | tf_op | source)
XLA Modules:
  0.0 793.5 jit_solution(851184003660964084)
XLA Ops:
  32.5 4.8 fusion.87
  40.4 6.1 multiply_convert_fusion.1
  46.6 6.5 fusion.84
  79.8 6.7 select_maximum_fusion.9
  86.5 609.8 %while.18 = (s32[]{:T(128)}, f32[27,10,18,130]{3,2,1,0:T(8,128)}, f32[27,10,18,130]{3,2,1,0:T(8,128)}, f32[2,2,2,10,18,130]{5,4,3,2,1,0:T(8,128)}, f32[2,2,2,10,...) while((s32[]{:T(128)}, f32[27,10,18,130]{3,2,1,0:T(8,128)}, ...), condition=%wide.region_3.4_spmd.clone.clone, body=%wide.region_2.3_spmd.clone.sunk.clone | while | flops 11477586 | bytes 82138408 | solution.py:153
  101.9 4.6 fusion.155
  124.5 4.6 fusion.155
  147.1 4.6 fusion.155
  169.7 4.6 fusion.155
  192.3 4.6 fusion.155
  214.9 4.6 fusion.155
  237.5 4.6 fusion.155
  260.1 4.6 fusion.155
  282.6 4.6 fusion.155
  305.2 4.6 fusion.155
  327.8 4.6 fusion.155
  350.4 4.6 fusion.155
  373.0 4.6 fusion.155
  395.6 4.6 fusion.155
  418.2 4.6 fusion.155
  440.7 4.6 fusion.155
  485.9 4.6 fusion.155
  508.4 4.6 fusion.155
  531.0 4.6 fusion.155
  576.2 4.6 fusion.155
  598.8 4.6 fusion.155
  643.9 4.6 fusion.155
  666.5 4.6 fusion.155
  689.1 4.6 fusion.155
  710.6 15.7 %scatter_fusion = f32[256,27,128]{2,1,0:T(8,128)} fusion(f32[256,27,128]{2,1,0:T(8,128)} %broadcast_in_dim.240, s32[128]{0:T(128)S(1)} %copy-done.36, f32[128,27,128]{2,1,0:T(8,128)S(1)} %bitcast.661), kind=kCustom, calls=%fused_computation | custom fusion | bytes 5308928 | tf_op jit(solution)/shard_map/scatter | solution.py:199
  726.2 5.6 copy.14
  731.9 57.7 %all_to_all.5 = f32[128,2,27,128]{3,1,2,0:T(2,128)S(1)} all-to-all(f32[128,2,27,128]{3,1,2,0:T(2,128)S(1)} %copy.14), channel_id=1, replica_groups=mesh['gx'=16,'gy'=8] {'gx','gy'}, dimensions={0} | all-to-all | bytes 7077888 | tf_op jit(solution)/shard_map/all_to_all | solution.py:202
  (2030 shorter events, 566.3 us)
Async XLA Ops:
  0.0 40.4 %copy-start = (bf16[128,27]{0,1:T(8,128)(2,1)S(1)}, bf16[128,27]{0,1:T(8,128)(2,1)}, u32[]{:S(2)}) copy-start(bf16[128,27]{0,1:T(8,128)(2,1)} %param.12) | copy-start | bytes 20740
  0.9 15.3 %collective-permute-start = (f32[2,2,2,1,16,128]{5,4,3,2,1,0:T(8,128)S(1)}, f32[2,2,2,1,16,128]{5,4,3,2,1,0:T(8,128)S(1)}, u32[]{:S(2)}, u32[]{:S(2)}) collective-permute-start(f32[2,2,2,1,16,128]{5,4,3,2,1,0:T(8,128)S(1)} %get-tuple-element.418), channel_id=1, source_target_pairs={{0,8},{8,16},{16,24},{24,32},{32,40},{40,48},{48,56},{56,64},{64,7... | collective-permute-start | bytes 196616 | tf_op jit(solution)/shard_map/ppermute | solution.py:14
  4.9 12.5 %collective-permute-start.1 = (f32[2,2,2,1,16,128]{5,4,3,2,1,0:T(8,128)S(1)}, f32[2,2,2,1,16,128]{5,4,3,2,1,0:T(8,128)S(1)}, u32[]{:S(2)}, u32[]{:S(2)}) collective-permute-start(f32[2,2,2,1,16,128]{5,4,3,2,1,0:T(8,128)S(1)} %get-tuple-element.417), channel_id=1, source_target_pairs={{8,0},{16,8},{24,16},{32,24},{40,32},{48,40},{56,48},{64,56},{72,6... | collective-permute-start | bytes 196616 | tf_op jit(solution)/shard_map/ppermute | solution.py:15
  17.4 6.9 collective-permute-start.2
  21.8 5.3 collective-permute-start.3
  55.3 7.8 collective-permute-start.4
  60.2 7.6 collective-permute-start.5
  69.4 6.5 collective-permute-start.6
  73.4 6.4 collective-permute-start.7
  99.7 7.3 slice-start.2
  122.3 7.3 slice-start.2
  144.9 7.3 slice-start.2
  167.5 7.3 slice-start.2
  190.1 7.3 slice-start.2
  212.7 7.3 slice-start.2
  235.2 7.3 slice-start.2
  257.8 7.3 slice-start.2
  280.4 7.3 slice-start.2
  303.0 7.3 slice-start.2
  325.6 7.3 slice-start.2
  348.2 7.3 slice-start.2
  370.8 7.3 slice-start.2
  393.4 7.3 slice-start.2
  415.9 7.3 slice-start.2
  438.5 7.3 slice-start.2
  461.1 7.3 slice-start.2
  528.8 7.3 slice-start.2
  551.4 7.3 slice-start.2
  619.2 7.3 slice-start.2
  641.7 7.3 slice-start.2
  664.3 7.3 slice-start.2
  731.9 61.4 %copy-start.1 = (bf16[128,27]{0,1:T(8,128)(2,1)S(1)}, bf16[128,27]{0,1:T(8,128)(2,1)}, u32[]{:S(2)}) copy-start(bf16[128,27]{0,1:T(8,128)(2,1)} %param.12) | copy-start | bytes 20740
  (285 other events, 804.1 us)
where the time goes:
time: 799 us; the launch traced here: 793 us
  other arithmetic  450 us (56%)
  local copies, waits for them, and re-layouts  225 us (28%)
  blocking collectives  57.7 us (7%)
  starting transfers between devices  23.1 us (3%)
  waiting for transfers between devices  12.8 us (2%)
  matrix products  12.7 us (2%)
  loops' own time  11.3 us (1%)
    add x27, other arithmetic, operate(): accumulated + step_minus(face, which_axis) * (field - step_minus(field, w...  125 us
    another operation x162, other arithmetic, prolong(): jnp.stack([jnp.stack([jnp.stack([parity_sums[parity_x, parity_y, parity_z...  123 us
    select_n x27, other arithmetic, probe(): masked = jnp.where(chosen[None], weights_ext, 0.0)  95.9 us
    while x432, local copies, waits for them, and re-layouts  63.4 us
    all_to_all x1, blocking collectives, per_device(): lax.all_to_all(outgoing, ('gx', 'gy'), split_axis=0, concat_axis=0, tiled...  57.7 us
    dynamic_update_slice x27, other arithmetic, probe(): lax.dynamic_update_index_in_dim(probe_stack, restrict(applied, weights_ex...  55 us
    slice x354, local copies, waits for them, and re-layouts, shift_prev(): lower_part = lax.slice_in_dim(values, 0, length - 1, axis=which_axis)  52.8 us
    slice x516, local copies, waits for them, and re-layouts, shift_next(): upper_part = lax.slice_in_dim(values, 1, length, axis=which_axis)  47 us
  transfers between devices with their start and end apart: 8, of which 4 were waited for; matrix products, arithmetic and copies ran while one was open for 2% of the time, Pallas kernels for 0%

commit v1 on v0

v1 whole, which is shorter than its diff:
```python
import functools

import jax
import jax.numpy as jnp
import numpy as np
from jax import lax
from jax.experimental import pallas as pl
from jax.experimental.pallas import tpu as pltpu
from jax.sharding import PartitionSpec as P

OFFSETS = [(a, b, c) for a in (-1, 0, 1) for b in (-1, 0, 1) for c in (-1, 0, 1)]
INNER = 27
PITCH = 28
YP = 32
Y0 = 8


def parity(o):
    return 4 * (o[0] != 0) + 2 * (o[1] != 0) + (o[2] != 0)


def tile_row(o):
    return 32 * (o[0] == -1) + 16 * (o[1] == -1) + 8 * (o[2] == -1) + parity(o)


def spread():
    m = np.zeros((27, 64), np.float32)
    for n, o in enumerate(OFFSETS):
        m[n, tile_row(o)] = 1.0
    return m


def z_before(v):
    lane = lax.broadcasted_iota(jnp.int32, v.shape, v.ndim - 1)
    return jnp.where(lane == 0, 0.0, pltpu.roll(v, 1, v.ndim - 1))


def z_after(v):
    lane = lax.broadcasted_iota(jnp.int32, v.shape, v.ndim - 1)
    last = v.shape[-1] - 1
    return jnp.where(lane == last, 0.0, pltpu.roll(v, last, v.ndim - 1))


def main_kernel(nx, ny, edge_ref, owner_ref, coef_ref, xlo_ref, xhi_ref, ylo_ref, yhi_ref,
                w1_ref, b1_ref, wm_ref, bm_ref, wo_ref, bo_ref, out_ref,
                k_ref, r_ref, f_ref, rt_ref, t_ref, u_ref, s_ref, count_ref):
    nz = 128
    ex, ey = nx + 3, ny + 3
    hx, hy = nx + 2, ny + 2
    kp = ex * YP
    up = hx * hy
    for p in range(8):
        k_ref[p, 2:2 + nx, Y0:Y0 + ny] = coef_ref[p]
        k_ref[p, 0:2, Y0:Y0 + ny] = xlo_ref[p]
        k_ref[p, 2 + nx:, Y0:Y0 + ny] = xhi_ref[p]
        for x in range(ex):
            k_ref[p, x, Y0 - 2:Y0] = ylo_ref[p, x]
            k_ref[p, x, Y0 + ny:Y0 + ny + 1] = yhi_ref[p, x]
    flat_k = k_ref.reshape(8 * kp, nz)
    flat_r = r_ref.reshape(8 * kp, nz)

    def roots(i, _):
        rows = pl.ds(pl.multiple_of(i * YP, YP), YP)
        flat_r[rows, :] = jnp.sqrt(flat_k[rows, :])
        return _

    lax.fori_loop(0, 8 * ex, roots, 0)

    def tiles(x, _):
        for y in range(ey):
            kt = flat_k[pl.ds(x * YP + Y0 - 2 + y, 8, stride=kp), :]
            logs = jnp.log(1.0 + kt)
            f_ref[x, y] = jnp.concatenate([logs, z_before(logs)], 0).astype(jnp.bfloat16)
            rt = jnp.sqrt(kt)
            rt_ref[x, y, 0:8] = rt
            rt_ref[x, y, 8:16] = z_before(rt)
        return _

    lax.fori_loop(0, ex, tiles, 0)

    def ratios(x, _):
        for blk in range(0, ny + 1, 8):
            rows = min(8, ny + 1 - blk)

            def at(px, py, pz, dx, dy):
                p = 4 * px + 2 * py + pz
                return flat_r[pl.ds(p * kp + (x + 1 + dx) * YP + Y0 - 1 + blk + dy, rows), :]

            for p in range(8):
                px, py, pz = p >> 2, (p >> 1) & 1, p & 1
                own = at(px, py, pz, 0, 0)
                total = at(1 - px, py, pz, 0, 0) + at(1 - px, py, pz, 1 if px else -1, 0)
                total += at(px, 1 - py, pz, 0, 0) + at(px, 1 - py, pz, 0, 1 if py else -1)
                beside = at(px, py, 1 - pz, 0, 0)
                total += beside + (z_after(beside) if pz else z_before(beside))
                t = jnp.where(own > 0.0, total / jnp.where(own > 0.0, own, 1.0), 0.0)
                t_ref[p, x, pl.ds(blk, rows), :] = t
                if pz:
                    t_ref[8 + p // 2, x, pl.ds(blk, rows), :] = z_before(t)
        return _

    lax.fori_loop(0, nx + 1, ratios, 0)

    group = 6

    def predict(x, _):
        for y0 in range(0, hy, group):
            parts = []
            for y in range(y0, y0 + group):
                parts.append(jnp.concatenate(
                    [f_ref[x + 1, y + 1], f_ref[x + 1, y], f_ref[x, y + 1], f_ref[x, y]], 0))
            h = jnp.concatenate(parts, 1)
            v = jnp.dot(w1_ref[...], h, preferred_element_type=jnp.float32) + b1_ref[...]
            h = (v + v * jnp.tanh(v)).astype(jnp.bfloat16)
            for m in range(2):
                v = jnp.dot(wm_ref[m], h, preferred_element_type=jnp.float32) + bm_ref[m]
                h = (v + v * jnp.tanh(v)).astype(jnp.bfloat16)
            v = jnp.dot(wo_ref[...], h, preferred_element_type=jnp.float32) + bo_ref[...]
            w = 0.25 + 0.25 * jnp.tanh(v)
            for y in range(y0, y0 + group):
                inside = jnp.logical_not(
                    jnp.logical_or(jnp.logical_and(x == hx - 1, edge_ref[0] == 1),
                                   jnp.logical_and(y == hy - 1, edge_ref[1] == 1)))
                keep = jnp.where(inside, 1.0, 0.0)
                wy = w[:, (y - y0) * nz:(y - y0 + 1) * nz] * keep
                for q, (sx, sy) in enumerate(((0, 0), (0, 1), (1, 0), (1, 1))):
                    for sz in range(2):
                        part = 16 * q + 8 * sz
                        u = wy[part:part + 8] * rt_ref[x + 1 - sx, y + 1 - sy, 8 * sz:8 * sz + 8]
                        at = part * up + x * hy + y
                        u_ref[0, pl.ds(at, 8, stride=up), :] = u
                        u_ref[1, pl.ds(at, 8, stride=up), :] = z_after(u)
                        if not sz:
                            u_ref[2, pl.ds(at, 8, stride=up), :] = z_before(u)
        return _

    lax.fori_loop(0, hx, predict, 0)

    def galerkin(x, _):
        for yb in range(0, ny, 8):

            def u_at(f, o):
                plane = tile_row(f)
                which = {0: 0, 1: 1, -1: 2}[o[2]]
                row = plane * up + (x + 1 + o[0]) * hy + yb + 1 + o[1]
                return u_ref[which, pl.ds(row, 8), :]

            own = {f: u_at(f, (0, 0, 0)) for f in OFFSETS}
            q = {}
            for f in OFFSETS:
                p = parity(f)
                plane = 8 + p // 2 if f[2] == -1 else p
                t = t_ref[plane, x + 1 - (f[0] == -1), pl.ds(yb + 1 - (f[1] == -1), 8), :]
                total = t * own[f]
                for d in range(3):
                    for step in (-1, 1):
                        g = tuple(f[n] + (step if n == d else 0) for n in range(3))
                        if g in own:
                            total = total - own[g]
                q[f] = total
            for n, o in enumerate(OFFSETS):
                plus = minus = None
                for fx in range(-2, 3):
                    for fy in range(-2, 3):
                        for fz in range(-2, 3):
                            f = (fx, fy, fz)
                            far = [d for d in range(3) if abs(f[d]) == 2]
                            g = tuple(f[d] - 2 * o[d] for d in range(3))
                            if len(far) > 1 or max(map(abs, g)) > 1:
                                continue
                            other = u_at(g, o)
                            if far:
                                near = tuple(v // 2 if d == far[0] else v for d, v in enumerate(f))
                                term = other * own[near]
                                minus = term if minus is None else minus + term
                            else:
                                term = other * q[f]
                                plus = term if plus is None else plus + term
                total = plus if minus is None else plus - minus
                s_ref[pl.ds(n * nx * ny + x * ny + yb, 8), :] = total
        return _

    lax.fori_loop(0, nx, galerkin, 0)

    def clear(i, _):
        out_ref[pl.ds(pl.multiple_of(i * 56, 8), 56), :] = jnp.zeros((56, nz), jnp.float32)
        count_ref[i] = 0
        return _

    lax.fori_loop(0, out_ref.shape[0] // 56, clear, 0)

    def place(x, _):
        for y in range(ny):
            who = owner_ref[x, y]
            rank = count_ref[who]
            count_ref[who] = rank + 1
            row = (who * 2 + rank) * PITCH
            c = x * ny + y
            for n in (0, 8, 16, 24):
                size = min(8, INNER - n)
                out_ref[pl.ds(row + n, size), :] = s_ref[pl.ds(n * nx * ny + c, size, stride=nx * ny), :]
        return _

    lax.fori_loop(0, nx, place, 0)


def unpack_kernel(in_ref, out_ref):
    slots = out_ref.shape[1]

    def one(o, _):
        for k in range(0, slots, 8):
            out_ref[o, pl.ds(k, 8), :] = in_ref[pl.ds(k * PITCH + o, 8, stride=PITCH), :]
        return _

    lax.fori_loop(0, out_ref.shape[0], one, 0)


def per_device(coefficient, owner, w_in, b_in, w_mid, b_mid, w_out, b_out):
    nx, ny, nz = coefficient.shape[3:]
    devices = lax.axis_size("gx") * lax.axis_size("gy")
    k = coefficient.reshape(8, nx, ny, nz)

    def send(v, axis, step):
        size = lax.axis_size(axis)
        pairs = [(i, i + step) for i in range(size) if 0 <= i + step < size]
        return lax.ppermute(v, axis, pairs)

    xlo = send(k[:, nx - 2:], "gx", 1)
    xhi = send(k[:, :1], "gx", -1)
    kx = lambda a, b: jnp.concatenate([xlo[:, :, a:b], k[:, :, a:b], xhi[:, :, a:b]], 1)
    ylo = send(kx(ny - 2, ny), "gy", 1)
    yhi = send(kx(0, 1), "gy", -1)

    spread_rows = jnp.asarray(spread(), jnp.bfloat16)
    w1 = jnp.dot(w_in * jnp.bfloat16(0.5), spread_rows, preferred_element_type=jnp.float32).astype(jnp.bfloat16)
    wo = jnp.dot(spread_rows.T, w_out * jnp.bfloat16(0.5), preferred_element_type=jnp.float32).astype(jnp.bfloat16)
    bo = jnp.dot(jnp.asarray(spread().T), b_out * 0.5, precision=lax.Precision.HIGHEST)
    edge = jnp.stack([lax.axis_index("gx") == lax.axis_size("gx") - 1,
                      lax.axis_index("gy") == lax.axis_size("gy") - 1]).astype(jnp.int32)
    ex, ey, hx, hy = nx + 3, ny + 3, nx + 2, ny + 2
    vmem = pl.BlockSpec(memory_space=pltpu.VMEM)
    smem = pl.BlockSpec(memory_space=pltpu.SMEM)
    out = pl.pallas_call(
        functools.partial(main_kernel, nx, ny),
        out_shape=jax.ShapeDtypeStruct((devices * 2 * PITCH, nz), jnp.float32),
        in_specs=[smem, smem] + [vmem] * 11,
        out_specs=vmem,
        scratch_shapes=[
            pltpu.VMEM((8, ex, YP, nz), jnp.float32),
            pltpu.VMEM((8, ex, YP, nz), jnp.float32),
            pltpu.VMEM((ex, ey, 16, nz), jnp.bfloat16),
            pltpu.VMEM((ex, ey, 16, nz), jnp.float32),
            pltpu.VMEM((12, nx + 1, 24, nz), jnp.float32),
            pltpu.VMEM((3, 64 * hx * hy, nz), jnp.float32),
            pltpu.VMEM((INNER * nx * ny, nz), jnp.float32),
            pltpu.SMEM((devices,), jnp.int32),
        ],
        compiler_params=pltpu.CompilerParams(vmem_limit_bytes=48 * 2**20),
        name="stencils",
    )(edge, owner, k, xlo, xhi, ylo, yhi, w1, b_in[:, None] * 0.5, w_mid * jnp.bfloat16(0.5),
      b_mid[:, :, None] * 0.5, wo, bo[:, None])
    got = lax.all_to_all(out.reshape(devices, 2 * PITCH, nz), ("gx", "gy"), split_axis=0, concat_axis=0, tiled=True)
    relaid = pl.pallas_call(
        unpack_kernel,
        out_shape=jax.ShapeDtypeStruct((27, devices * 2, nz), jnp.float32),
        in_specs=[vmem],
        out_specs=vmem,
        compiler_params=pltpu.CompilerParams(vmem_limit_bytes=32 * 2**20),
        name="unpack",
    )(got.reshape(devices * 2 * PITCH, nz))
    return jnp.transpose(relaid, (1, 0, 2))


def solution(mesh):
    return jax.shard_map(
        per_device,
        mesh=mesh,
        in_specs=(P(None, None, None, "gx", "gy", None), P("gx", "gy"), P(), P(), P(), P(), P(), P()),
        out_specs=P(("gx", "gy"), None, None),
        check_vma=False,
    )
```

time: 799 us -> 115 us (0.14)
  other arithmetic: 450 us -> 2.36 us
  local copies, waits for them, and re-layouts: 225 us -> 5.83 us
  Pallas kernels: 0 us -> 29.6 us
  waiting for transfers between devices: 12.8 us -> 1.08 us
  loops' own time: 11.3 us -> 0 us
  starting transfers between devices: 23.1 us -> 12.7 us
  matrix products: 12.7 us -> 2.75 us
    another operation x298 -> x0, other arithmetic: 140 us -> none  [the longest x162 123 us: prolong(): jnp.stack([jnp.stack([jnp.stack([parity_sums[parity_x, parity_y, parity_z...]
    add x30 -> x0, other arithmetic: 130 us -> none  [the longest x27 125 us: operate(): accumulated + step_minus(face, which_axis) * (field - step_minus(field, w...]
    slice x964 -> x8, local copies, waits for them, and re-layouts: 113 us -> 3.74 us  [the longest x2 1.95 us: per_device(): k[:, :, a:b]]
    select_n x28 -> x0, other arithmetic: 96.5 us -> none  [the longest x27 95.9 us: probe(): masked = jnp.where(chosen[None], weights_ext, 0.0)]
    while x432 -> x0, local copies, waits for them, and re-layouts: 63.4 us -> none
    dynamic_update_slice x27 -> x0, other arithmetic: 55 us -> none  [probe(): lax.dynamic_update_index_in_dim(probe_stack, restrict(applied, weights_ex...]
    pallas_call x0 -> x2, Pallas kernels: none -> 29.6 us  [the longest x1 27.3 us: per_device(): pl.pallas_call(functools.partial(main_kernel, nx, ny), out_shape=jax.Shap...]
    scatter x1 -> x0, local copies, waits for them, and re-layouts: 15.7 us -> none  [per_device(): jnp.zeros((devices * per_pair, points, depth), jnp.float32).at[slot_index]]
  transfers between devices with their start and end apart: 8 -> 4, of which waited for: 4 -> 1; matrix products, arithmetic and copies ran while one was open for 2% -> 7% of each run, Pallas kernels for 0% -> 0%
where the time goes in v1:
time: 115 us; the launch traced here: 114 us
  blocking collectives  59.6 us (52%)
  Pallas kernels  29.6 us (26%)
  starting transfers between devices  12.7 us (11%)
  local copies, waits for them, and re-layouts  5.83 us (5%)
  matrix products  2.75 us (2%)
  other arithmetic  2.36 us (2%)
    all_to_all x1, blocking collectives, per_device(): lax.all_to_all(out.reshape(devices, 2 * PITCH, nz), ('gx', 'gy'), split_a...  59.6 us
    pallas_call x1, Pallas kernels, per_device(): pl.pallas_call(functools.partial(main_kernel, nx, ny), out_shape=jax.Shap...  27.3 us
    ppermute x4, starting transfers between devices, send(): return lax.ppermute(v, axis, pairs)  12.7 us
  transfers between devices with their start and end apart: 4, of which 1 were waited for; matrix products, arithmetic and copies ran while one was open for 7% of the time, Pallas kernels for 0%

profile of v1, /device:TPU:1, one launch (start us, length us, event | category | flops | bytes accessed | tf_op | source)
XLA Modules:
  0.0 114.0 jit_solution(18370131556444230942)
XLA Ops:
  0.0 0.8 slice.33
  0.8 1.3 %collective-permute-start.1 = (f32[8,1,16,128]{3,2,1,0:T(8,128)S(1)}, f32[8,1,16,128]{3,2,1,0:T(8,128)S(1)}, u32[]{:S(2)}, u32[]{:S(2)}) collective-permute-start(f32[8,1,16,128]{3,2,1,0:T(8,128)S(1)} %slice.33), channel_id=1, source_target_pairs={{8,0},{16,8},{24,16},{32,24},{40,32},{48,40},{56,48},{64,56},{72,6... | collective-permute-start | bytes 196616 | tf_op jit(solution)/shard_map/ppermute | solution.py:226
  2.1 0.9 slice.32
  3.1 4.6 %collective-permute-start = (f32[8,2,16,128]{3,2,1,0:T(8,128)S(1)}, f32[8,2,16,128]{3,2,1,0:T(8,128)S(1)}, u32[]{:S(2)}, u32[]{:S(2)}) collective-permute-start(f32[8,2,16,128]{3,2,1,0:T(8,128)S(1)} %slice.32), channel_id=1, source_target_pairs={{0,8},{8,16},{16,24},{24,32},{32,40},{40,48},{48,56},{56,64},{64,7... | collective-permute-start | bytes 393224 | tf_op jit(solution)/shard_map/ppermute | solution.py:226
  7.6 0.7 multiply_bitcast_fusion
  8.3 0.9 convolution_convert_fusion.1
  9.2 0.9 fusion.wo_ref
  10.2 0.9 broadcast_multiply_fusion.wm_ref
  11.0 0.9 convolution_bitcast_fusion.bo_ref
  11.9 0.7 multiply_bitcast_fusion.1
  12.6 1.0 slice.38
  13.6 1.0 slice.35
  14.6 0.0 collective-permute-done.1.xhi_ref
  14.6 0.0 collective-permute-done.xlo_ref
  14.7 3.3 %collective-permute-start.3 = (f32[8,11,1,128]{3,2,1,0:T(1,128)S(1)}, f32[8,11,1,128]{3,2,1,0:T(1,128)S(1)}, u32[]{:S(2)}, u32[]{:S(2)}) collective-permute-start(f32[8,11,1,128]{3,2,1,0:T(1,128)S(1)} %pad_maximum_fusion.1), channel_id=1, source_target_pairs={{1,0},{2,1},{3,2},{4,3},{5,4},{6,5},{7,6},{9,8},{10,9},{11,10},{12... | collective-permute-start | bytes 135176 | tf_op jit(solution)/shard_map/ppermute | solution.py:226
  18.1 3.5 %collective-permute-start.2 = (f32[8,11,2,128]{3,2,1,0:T(2,128)S(1)}, f32[8,11,2,128]{3,2,1,0:T(2,128)S(1)}, u32[]{:S(2)}, u32[]{:S(2)}) collective-permute-start(f32[8,11,2,128]{3,2,1,0:T(2,128)S(1)} %pad_maximum_fusion), channel_id=1, source_target_pairs={{0,1},{1,2},{2,3},{3,4},{4,5},{5,6},{6,7},{8,9},{9,10},{10,11},{11... | collective-permute-start | bytes 270344 | tf_op jit(solution)/shard_map/ppermute | solution.py:226
  21.6 0.1 add_convert_fusion.edge_ref
  21.7 0.1 copy.18.w1_ref
  21.8 0.1 copy.19.b1_ref
  21.9 0.1 copy.20.bm_ref
  22.1 0.0 collective-permute-done.3.yhi_ref
  22.1 1.1 collective-permute-done.2.ylo_ref
  23.1 0.0 copy-start
  23.1 1.0 copy-done
  24.2 0.0 copy-start.1
  24.2 0.7 copy-done.1
  24.9 27.3 %stencils.1 = f32[7168,128]{1,0:T(8,128)S(1)} custom-call(s32[2]{0:T(128)S(1)} %add_convert_fusion.edge_ref, s32[8,16]{1,0:T(8,128)S(1)} %copy-done.1, f32[8,8,16,128]{3,2,1,0:T(8,128)S(1)} %bitcast.28, f32[8,2,16,128]{3,2,1,0:T(8,128)S(1)} %collective-permute-done.xlo_ref, f32[8,1,16,128]{3,2,1,0:T(8,128)S(1)} %collective-permute-done.1.xhi_ref, ...), custom_call_target="tpu_custom_call" | custom-call | tf_op jit(solution)/shard_map/stencils/pallas_call | solution.py:243
  52.2 59.6 %all_to_all.5 = f32[128,56,128]{2,1,0:T(8,128)S(1)} all-to-all(f32[128,56,128]{2,1,0:T(8,128)S(1)} %bitcast.22), channel_id=1, replica_groups=mesh['gx'=16,'gy'=8] {'gx','gy'}, dimensions={0} | all-to-all | bytes 7340032 | tf_op jit(solution)/shard_map/all_to_all | solution.py:262
  111.7 2.3 %unpack.1 = f32[27,256,128]{2,1,0:T(8,128)} custom-call(f32[7168,128]{1,0:T(8,128)S(1)} %bitcast.23), custom_call_target="tpu_custom_call" | custom-call | tf_op jit(solution)/shard_map/unpack/pallas_call | solution.py:263
  (6 shorter events, 0.1 us)
Async XLA Ops:
  0.8 13.7 %collective-permute-start.1 = (f32[8,1,16,128]{3,2,1,0:T(8,128)S(1)}, f32[8,1,16,128]{3,2,1,0:T(8,128)S(1)}, u32[]{:S(2)}, u32[]{:S(2)}) collective-permute-start(f32[8,1,16,128]{3,2,1,0:T(8,128)S(1)} %slice.33), channel_id=1, source_target_pairs={{8,0},{16,8},{24,16},{32,24},{40,32},{48,40},{56,48},{64,56},{72,6... | collective-permute-start | bytes 196616 | tf_op jit(solution)/shard_map/ppermute | solution.py:226
  3.1 11.6 %collective-permute-start = (f32[8,2,16,128]{3,2,1,0:T(8,128)S(1)}, f32[8,2,16,128]{3,2,1,0:T(8,128)S(1)}, u32[]{:S(2)}, u32[]{:S(2)}) collective-permute-start(f32[8,2,16,128]{3,2,1,0:T(8,128)S(1)} %slice.32), channel_id=1, source_target_pairs={{0,8},{8,16},{16,24},{24,32},{32,40},{40,48},{48,56},{56,64},{64,7... | collective-permute-start | bytes 393224 | tf_op jit(solution)/shard_map/ppermute | solution.py:226
  14.7 7.4 %collective-permute-start.3 = (f32[8,11,1,128]{3,2,1,0:T(1,128)S(1)}, f32[8,11,1,128]{3,2,1,0:T(1,128)S(1)}, u32[]{:S(2)}, u32[]{:S(2)}) collective-permute-start(f32[8,11,1,128]{3,2,1,0:T(1,128)S(1)} %pad_maximum_fusion.1), channel_id=1, source_target_pairs={{1,0},{2,1},{3,2},{4,3},{5,4},{6,5},{7,6},{9,8},{10,9},{11,10},{12... | collective-permute-start | bytes 135176 | tf_op jit(solution)/shard_map/ppermute | solution.py:226
  18.1 5.1 %collective-permute-start.2 = (f32[8,11,2,128]{3,2,1,0:T(2,128)S(1)}, f32[8,11,2,128]{3,2,1,0:T(2,128)S(1)}, u32[]{:S(2)}, u32[]{:S(2)}) collective-permute-start(f32[8,11,2,128]{3,2,1,0:T(2,128)S(1)} %pad_maximum_fusion), channel_id=1, source_target_pairs={{0,1},{1,2},{2,3},{3,4},{4,5},{5,6},{6,7},{8,9},{9,10},{10,11},{11... | collective-permute-start | bytes 270344 | tf_op jit(solution)/shard_map/ppermute | solution.py:226
  23.1 1.0 copy-start
  24.2 0.7 copy-start.1

commit v2 on v1

v2 whole, which is shorter than its diff:
```python
import functools

import jax
import jax.numpy as jnp
from jax import lax
from jax.experimental import pallas as pl
from jax.experimental.pallas import tpu as pltpu
from jax.sharding import PartitionSpec as P

OFFSETS = [(a, b, c) for a in (-1, 0, 1) for b in (-1, 0, 1) for c in (-1, 0, 1)]
SENT = [o for o in OFFSETS if o != (0, 0, -1)]
PITCH = len(SENT)
YP = 32
Y0 = 8


def parity(o):
    return 4 * (o[0] != 0) + 2 * (o[1] != 0) + (o[2] != 0)


def tile_row(o):
    return 32 * (o[0] == -1) + 16 * (o[1] == -1) + 8 * (o[2] == -1) + parity(o)


def offset_of_row(shape, dim):
    row = lax.broadcasted_iota(jnp.int32, shape, dim)
    number = jnp.zeros(shape, jnp.int32)
    none = jnp.zeros(shape, jnp.bool_)
    for lower, odd, scale in ((5, 2, 9), (4, 1, 3), (3, 0, 1)):
        low, away = (row >> lower) & 1, (row >> odd) & 1
        number += (1 + away - 2 * low) * scale
        none = jnp.logical_or(none, low > away)
    return jnp.where(none, -1, number)


def as_column(row, chosen):
    return jnp.sum(jnp.where(chosen, row, 0.0), axis=1, keepdims=True)


def z_before(v):
    lane = lax.broadcasted_iota(jnp.int32, v.shape, v.ndim - 1)
    return jnp.where(lane == 0, 0.0, pltpu.roll(v, 1, v.ndim - 1))


def z_after(v):
    lane = lax.broadcasted_iota(jnp.int32, v.shape, v.ndim - 1)
    last = v.shape[-1] - 1
    return jnp.where(lane == last, 0.0, pltpu.roll(v, last, v.ndim - 1))


def send_x_kernel(k_ref, up_ref, down_ref):
    nx = k_ref.shape[1]
    up_ref[...] = k_ref[:, nx - 2:]
    down_ref[...] = k_ref[:, :1]


def send_y_kernel(k_ref, xlo_ref, xhi_ref, up_ref, down_ref):
    nx, ny = k_ref.shape[1:3]
    for to, rows in ((up_ref, slice(ny - 2, ny)), (down_ref, slice(0, 1))):
        to[:, 0:2] = xlo_ref[:, :, rows]
        to[:, 2:2 + nx] = k_ref[:, :, rows]
        to[:, 2 + nx:] = xhi_ref[:, :, rows]


def feature_tile(kt):
    logs = jnp.log(1.0 + kt)
    return jnp.concatenate([logs, z_before(logs)], 0).astype(jnp.bfloat16)


def mlp(f, columns, layers):
    w1_ref, b1_ref, wm_ref, bm_ref, wo_ref, bo_ref = layers
    h = jnp.concatenate(
        [jnp.concatenate([f(x, y), f(x, y - 1), f(x - 1, y), f(x - 1, y - 1)], 0) for x, y in columns], 1)
    v = jnp.dot(w1_ref[...], h, preferred_element_type=jnp.float32) + b1_ref[...]
    h = (v + v * jnp.tanh(v)).astype(jnp.bfloat16)
    for m in range(2):
        v = jnp.dot(wm_ref[m], h, preferred_element_type=jnp.float32) + bm_ref[m]
        h = (v + v * jnp.tanh(v)).astype(jnp.bfloat16)
    v = jnp.dot(wo_ref[...], h, preferred_element_type=jnp.float32) + bo_ref[...]
    return 0.25 + 0.25 * jnp.tanh(v)


def inner_kernel(nx, ny, k_ref, win_ref, bin_ref, wmid_ref, bmid_ref, wout_ref, bout_ref,
                 w1_ref, b1_ref, wm_ref, bm_ref, wo_ref, bo_ref, w_ref, f_ref):
    nz = 128
    half = jnp.bfloat16(0.5)
    eye = lax.broadcasted_iota(jnp.int32, (128, 128), 0) == lax.broadcasted_iota(jnp.int32, (128, 128), 1)
    into = offset_of_row((27, 64), 1) == lax.broadcasted_iota(jnp.int32, (27, 64), 0)
    out_of = offset_of_row((64, 27), 0) == lax.broadcasted_iota(jnp.int32, (64, 27), 1)
    ones = lambda m: jnp.where(m, 1.0, 0.0).astype(jnp.bfloat16)
    w1_ref[...] = jnp.dot(win_ref[...] * half, ones(into), preferred_element_type=jnp.float32).astype(jnp.bfloat16)
    wo_ref[...] = jnp.dot(ones(out_of), wout_ref[...] * half, preferred_element_type=jnp.float32).astype(jnp.bfloat16)
    b1_ref[...] = as_column(bin_ref[...], eye) * 0.5
    bo_ref[...] = as_column(bout_ref[...], out_of) * 0.5
    for m in range(2):
        wm_ref[m] = wmid_ref[m] * half
        bm_ref[m] = as_column(bmid_ref[m:m + 1], eye) * 0.5
    layers = (w1_ref, b1_ref, wm_ref, bm_ref, wo_ref, bo_ref)
    flat = k_ref.reshape(8 * nx * ny, nz)

    def tiles(x, _):
        for y in range(ny):
            f_ref[x, y] = feature_tile(flat[pl.ds(x * ny + y, 8, stride=nx * ny), :])
        return _

    lax.fori_loop(0, nx, tiles, 0)

    def row(x, _):
        w = mlp(lambda a, b: f_ref[a, b], [(x, y) for y in range(1, ny)], layers)
        for y in range(1, ny):
            w_ref[(x - 1) * (ny - 1) + y - 1] = w[:, (y - 1) * nz:y * nz]
        return _

    lax.fori_loop(1, nx, row, 0)


def side_kernel(nx, ny, k_ref, xlo_ref, xhi_ref, w1_ref, b1_ref, wm_ref, bm_ref, wo_ref, bo_ref, w_ref, k5_ref, f_ref):
    nz = 128
    layers = (w1_ref, b1_ref, wm_ref, bm_ref, wo_ref, bo_ref)
    k5_ref[:, 0:2] = xlo_ref[...]
    k5_ref[:, 2:3] = k_ref[:, 0:1]
    k5_ref[:, 3:4] = k_ref[:, nx - 1:]
    k5_ref[:, 4:5] = xhi_ref[...]
    flat = k5_ref.reshape(8 * 5 * ny, nz)

    def tiles(x, _):
        for y in range(ny):
            f_ref[x, y] = feature_tile(flat[pl.ds(x * ny + y, 8, stride=5 * ny), :])
        return _

    lax.fori_loop(0, 5, tiles, 0)

    def row(i, _):
        x = jnp.where(i == 2, 4, i + 1)
        w = mlp(lambda a, b: f_ref[a, b], [(x, y) for y in range(1, ny)], layers)
        for y in range(1, ny):
            w_ref[i * (ny - 1) + y - 1] = w[:, (y - 1) * nz:y * nz]
        return _

    lax.fori_loop(0, 3, row, 0)


def main_kernel(nx, ny, owner_ref, coef_ref, xlo_ref, xhi_ref, ylo_ref, yhi_ref,
                w1_ref, b1_ref, wm_ref, bm_ref, wo_ref, bo_ref, inner_ref, side_ref, out_ref,
                k_ref, r_ref, f_ref, rt_ref, t_ref, u_ref, s_ref, count_ref):
    nz = 128
    layers = (w1_ref, b1_ref, wm_ref, bm_ref, wo_ref, bo_ref)
    ex, ey = nx + 3, ny + 3
    hx, hy = nx + 2, ny + 2
    kp = ex * YP
    up = hx * hy
    last_x = lax.axis_index("gx") == lax.axis_size("gx") - 1
    last_y = lax.axis_index("gy") == lax.axis_size("gy") - 1

    for p in range(8):
        k_ref[p, 2:2 + nx, Y0:Y0 + ny] = coef_ref[p]
        k_ref[p, 0:2, Y0:Y0 + ny] = xlo_ref[p]
        k_ref[p, 2 + nx:, Y0:Y0 + ny] = xhi_ref[p]
        for x in range(ex):
            k_ref[p, x, Y0 - 2:Y0] = ylo_ref[p, x]
            k_ref[p, x, Y0 + ny:Y0 + ny + 1] = yhi_ref[p, x]
    flat_k = k_ref.reshape(8 * kp, nz)
    flat_r = r_ref.reshape(8 * kp, nz)

    def roots(i, _):
        rows = pl.ds(pl.multiple_of(i * YP, YP), YP)
        flat_r[rows, :] = jnp.sqrt(flat_k[rows, :])
        return _

    lax.fori_loop(0, 8 * ex, roots, 0)

    rim = {0: 0, 1: 1, 2: 2, ey - 2: 3, ey - 1: 4}

    def tiles(x, _):
        for y in range(ey):
            at = pl.ds(x * YP + Y0 - 2 + y, 8, stride=kp)
            if y in rim:
                f_ref[x, rim[y]] = feature_tile(flat_k[at, :])
            rt = flat_r[at, :]
            rt_ref[x, y, 0:8] = rt
            rt_ref[x, y, 8:16] = z_before(rt)
        return _

    lax.fori_loop(0, ex, tiles, 0)

    def ratios(x, _):
        for blk in range(0, ny + 1, 8):
            rows = min(8, ny + 1 - blk)

            def at(px, py, pz, dx, dy):
                p = 4 * px + 2 * py + pz
                return flat_r[pl.ds(p * kp + (x + 1 + dx) * YP + Y0 - 1 + blk + dy, rows), :]

            for p in range(8):
                px, py, pz = p >> 2, (p >> 1) & 1, p & 1
                own = at(px, py, pz, 0, 0)
                total = at(1 - px, py, pz, 0, 0) + at(1 - px, py, pz, 1 if px else -1, 0)
                total += at(px, 1 - py, pz, 0, 0) + at(px, 1 - py, pz, 0, 1 if py else -1)
                beside = at(px, py, 1 - pz, 0, 0)
                total += beside + (z_after(beside) if pz else z_before(beside))
                t = jnp.where(own > 0.0, total / jnp.where(own > 0.0, own, 1.0), 0.0)
                t_ref[p, x, pl.ds(blk, rows), :] = t
                if pz:
                    t_ref[8 + p // 2, x, pl.ds(blk, rows), :] = z_before(t)
        return _

    lax.fori_loop(0, nx + 1, ratios, 0)

    def put(x, y, wy):
        for q, (sx, sy) in enumerate(((0, 0), (0, 1), (1, 0), (1, 1))):
            for sz in range(2):
                part = 16 * q + 8 * sz
                u = wy[part:part + 8] * rt_ref[x + 1 - sx, y + 1 - sy, 8 * sz:8 * sz + 8]
                at = part * up + x * hy + y
                u_ref[0, pl.ds(at, 8, stride=up), :] = u
                u_ref[1, pl.ds(at, 8, stride=up), :] = z_after(u)
                if not sz:
                    u_ref[2, pl.ds(at, 8, stride=up), :] = z_before(u)

    def put_inner(x, _):
        for y in range(1, ny):
            put(x + 1, y + 1, inner_ref[(x - 1) * (ny - 1) + y - 1])
        return _

    lax.fori_loop(1, nx, put_inner, 0)

    def put_side(i, _):
        keep = jnp.where(jnp.logical_and(i == 2, last_x), 0.0, 1.0)
        for y in range(1, ny):
            put(jnp.where(i == 2, hx - 1, i), y + 1, side_ref[i * (ny - 1) + y - 1] * keep)
        return _

    lax.fori_loop(0, 3, put_side, 0)
    columns = [(x, y) for y in (0, 1, hy - 1) for x in range(hx)]
    w = mlp(lambda x, y: f_ref[x, rim[y]], [(x + 1, y + 1) for x, y in columns], layers)
    for n, (x, y) in enumerate(columns):
        wy = w[:, n * nz:(n + 1) * nz]
        if x == hx - 1:
            wy = wy * jnp.where(last_x, 0.0, 1.0)
        if y == hy - 1:
            wy = wy * jnp.where(last_y, 0.0, 1.0)
        put(x, y, wy)

    def galerkin(x, _):
        for yb in range(0, ny, 8):

            def u_at(f, o):
                plane = tile_row(f)
                which = {0: 0, 1: 1, -1: 2}[o[2]]
                row = plane * up + (x + 1 + o[0]) * hy + yb + 1 + o[1]
                return u_ref[which, pl.ds(row, 8), :]

            own = {f: u_at(f, (0, 0, 0)) for f in OFFSETS}
            q = {}
            for f in OFFSETS:
                p = parity(f)
                plane = 8 + p // 2 if f[2] == -1 else p
                t = t_ref[plane, x + 1 - (f[0] == -1), pl.ds(yb + 1 - (f[1] == -1), 8), :]
                total = t * own[f]
                for d in range(3):
                    for step in (-1, 1):
                        g = tuple(f[n] + (step if n == d else 0) for n in range(3))
                        if g in own:
                            total = total - own[g]
                q[f] = total
            for n, o in enumerate(SENT):
                plus = minus = None
                for fx in range(-2, 3):
                    for fy in range(-2, 3):
                        for fz in range(-2, 3):
                            f = (fx, fy, fz)
                            far = [d for d in range(3) if abs(f[d]) == 2]
                            g = tuple(f[d] - 2 * o[d] for d in range(3))
                            if len(far) > 1 or max(map(abs, g)) > 1:
                                continue
                            other = u_at(g, o)
                            if far:
                                near = tuple(v // 2 if d == far[0] else v for d, v in enumerate(f))
                                term = other * own[near]
                                minus = term if minus is None else minus + term
                            else:
                                term = other * q[f]
                                plus = term if plus is None else plus + term
                total = plus if minus is None else plus - minus
                s_ref[pl.ds(n * nx * ny + x * ny + yb, 8), :] = total
        return _

    lax.fori_loop(0, nx, galerkin, 0)

    def clear(i, _):
        rows = 2 * 2 * PITCH
        out_ref[pl.ds(pl.multiple_of(i * rows, 8), rows), :] = jnp.zeros((rows, nz), jnp.float32)
        count_ref[2 * i] = 0
        count_ref[2 * i + 1] = 0
        return _

    lax.fori_loop(0, out_ref.shape[0] // (2 * 2 * PITCH), clear, 0)

    def place(x, _):
        for y in range(ny):
            who = owner_ref[x, y]
            rank = count_ref[who]
            count_ref[who] = rank + 1
            row = (who * 2 + rank) * PITCH
            c = x * ny + y
            for n in (0, 8, 16, 24):
                size = min(8, PITCH - n)
                out_ref[pl.ds(row + n, size), :] = s_ref[pl.ds(n * nx * ny + c, size, stride=nx * ny), :]
        return _

    lax.fori_loop(0, nx, place, 0)


def unpack_kernel(in_ref, out_ref):
    group, slots = out_ref.shape[:2]
    below, above = OFFSETS.index((0, 0, -1)), SENT.index((0, 0, 1))
    first = pl.program_id(0) * group

    def one(i, _):
        o = first + i
        n = jnp.where(o > below, o - 1, o)
        for k in range(0, slots, 8):
            out_ref[i, pl.ds(k, 8), :] = in_ref[pl.ds(k * PITCH + n, 8, stride=PITCH), :]
        return _

    lax.fori_loop(0, group, one, 0)

    @pl.when(pl.program_id(0) == below // group)
    def _():
        for k in range(0, slots, 8):
            out_ref[below % group, pl.ds(k, 8), :] = z_before(in_ref[pl.ds(k * PITCH + above, 8, stride=PITCH), :])


def per_device(coefficient, owner, w_in, b_in, w_mid, b_mid, w_out, b_out):
    nx, ny, nz = coefficient.shape[3:]
    devices = lax.axis_size("gx") * lax.axis_size("gy")
    k = coefficient.reshape(8, nx, ny, nz)
    ex, ey, hx, hy = nx + 3, ny + 3, nx + 2, ny + 2
    vmem = pl.BlockSpec(memory_space=pltpu.VMEM)
    smem = pl.BlockSpec(memory_space=pltpu.SMEM)
    f32 = lambda *shape: jax.ShapeDtypeStruct(shape, jnp.float32)
    bf16 = lambda *shape: jax.ShapeDtypeStruct(shape, jnp.bfloat16)

    def call(kernel, name, out_shape, args, scratch=(), limit=48, us=1, first=vmem):
        return pl.pallas_call(
            kernel,
            out_shape=out_shape,
            in_specs=[first] + [vmem] * (len(args) - 1),
            out_specs=jax.tree.map(lambda _: vmem, out_shape),
            scratch_shapes=scratch,
            compiler_params=pltpu.CompilerParams(vmem_limit_bytes=limit * 2**20),
            cost_estimate=pl.CostEstimate(flops=us * 10**9, bytes_accessed=2**20, transcendentals=0),
            name=name,
        )(*args)

    def send(v, axis, step):
        size = lax.axis_size(axis)
        pairs = [(i, i + step) for i in range(size) if 0 <= i + step < size]
        return lax.ppermute(v, axis, pairs)

    up, down = call(send_x_kernel, "send_x", (f32(8, 2, ny, nz), f32(8, 1, ny, nz)), (k,))
    xlo, xhi = send(up, "gx", 1), send(down, "gx", -1)
    up, down = call(send_y_kernel, "send_y", (f32(8, ex, 2, nz), f32(8, ex, 1, nz)), (k, xlo, xhi))
    ylo, yhi = send(up, "gy", 1), send(down, "gy", -1)
    *layers, inner = call(
        functools.partial(inner_kernel, nx, ny), "inner",
        (bf16(128, 64), f32(128, 1), bf16(2, 128, 128), f32(2, 128, 1), bf16(64, 128), f32(64, 1),
         f32((nx - 1) * (ny - 1), 64, nz)),
        (k, w_in, b_in[None], w_mid, b_mid, w_out, b_out[None]),
        scratch=[pltpu.VMEM((nx, ny, 16, nz), jnp.bfloat16)], us=7)
    side = call(
        functools.partial(side_kernel, nx, ny), "side", f32(3 * (ny - 1), 64, nz), (k, xlo, xhi, *layers),
        scratch=[pltpu.VMEM((8, 5, ny, nz), jnp.float32), pltpu.VMEM((5, ny, 16, nz), jnp.bfloat16)], us=4)
    out = call(
        functools.partial(main_kernel, nx, ny), "stencils", f32(devices * 2 * PITCH, nz),
        (owner, k, xlo, xhi, ylo, yhi, *layers, inner, side), us=12, first=smem,
        scratch=[
            pltpu.VMEM((8, ex, YP, nz), jnp.float32),
            pltpu.VMEM((8, ex, YP, nz), jnp.float32),
            pltpu.VMEM((ex, 5, 16, nz), jnp.bfloat16),
            pltpu.VMEM((ex, ey, 16, nz), jnp.float32),
            pltpu.VMEM((12, nx + 1, 24, nz), jnp.float32),
            pltpu.VMEM((3, 64 * hx * hy, nz), jnp.float32),
            pltpu.VMEM((PITCH * nx * ny, nz), jnp.float32),
            pltpu.SMEM((devices,), jnp.int32),
        ])
    got = lax.all_to_all(out.reshape(devices, -1, 4, nz), ("gx", "gy"), split_axis=0, concat_axis=0, tiled=True)
    relaid = pl.pallas_call(
        unpack_kernel,
        grid=(3,),
        out_shape=f32(27, devices * 2, nz),
        in_specs=[vmem],
        out_specs=pl.BlockSpec((9, devices * 2, nz), lambda i: (i, 0, 0)),
        compiler_params=pltpu.CompilerParams(vmem_limit_bytes=32 * 2**20),
        name="unpack",
    )(got.reshape(devices * 2 * PITCH, nz))
    return jnp.transpose(relaid, (1, 0, 2))


def solution(mesh):
    return jax.shard_map(
        per_device,
        mesh=mesh,
        in_specs=(P(None, None, None, "gx", "gy", None), P("gx", "gy"), P(), P(), P(), P(), P(), P()),
        out_specs=P(("gx", "gy"), None, None),
        check_vma=False,
    )
```

time: 115 us -> 97.5 us (0.85)
  blocking collectives: 59.6 us -> 55.5 us
  Pallas kernels: 29.6 us -> 25.7 us
  local copies, waits for them, and re-layouts: 5.83 us -> 2.89 us
  matrix products: 2.75 us -> 0 us
  other arithmetic: 2.36 us -> 0 us
    all_to_all x1, blocking collectives: 59.6 us -> 55.5 us  [per_device(): lax.all_to_all(out.reshape(devices, -1, 4, nz), ('gx', 'gy'), split_axis=...]
    pallas_call x2 -> x6, Pallas kernels: 29.6 us -> 25.7 us  [the longest x5 23.5 us: call(): pl.pallas_call(kernel, out_shape=out_shape, in_specs=[first] + [vmem] * (...]
    slice x8 -> x0, local copies, waits for them, and re-layouts: 3.74 us -> none  [the longest x2 1.95 us: per_device(): k[:, :, a:b]]
    dot_general x3 -> x0, matrix products: 2.75 us -> none  [the longest x1 0.93 us: per_device(): jnp.dot(jnp.asarray(spread().T), b_out * 0.5, precision=lax.Precision.HIG...]
    mul x3 -> x0, other arithmetic: 2.2 us -> none  [the longest x1 0.85 us: per_device(): w_mid * jnp.bfloat16(0.5)]
    unnamed x4 -> x21, local copies, waits for them, and re-layouts: 1.73 us -> 2.89 us
  transfers between devices with their start and end apart: 4 -> 4, of which waited for: 1 -> 0; matrix products, arithmetic and copies ran while one was open for 7% -> 0% of each run, Pallas kernels for 0% -> 10%
where the time goes in v2:
time: 97.5 us; the launch traced here: 97.2 us
  blocking collectives  55.5 us (57%)
  Pallas kernels  25.7 us (26%)
  starting transfers between devices  12.8 us (13%)
  local copies, waits for them, and re-layouts  2.89 us (3%)
    all_to_all x1, blocking collectives, per_device(): lax.all_to_all(out.reshape(devices, -1, 4, nz), ('gx', 'gy'), split_axis=...  55.5 us
    pallas_call x5, Pallas kernels, call(): pl.pallas_call(kernel, out_shape=out_shape, in_specs=[first] + [vmem] * (...  23.5 us
    ppermute x4, starting transfers between devices, send(): return lax.ppermute(v, axis, pairs)  12.8 us
    unnamed x21, local copies, waits for them, and re-layouts  2.89 us
    pallas_call x1, Pallas kernels, per_device(): pl.pallas_call(unpack_kernel, grid=(3,), out_shape=f32(27, devices * 2, n...  2.28 us
  transfers between devices with their start and end apart: 4, of which 0 were waited for; matrix products, arithmetic and copies ran while one was open for 0% of the time, Pallas kernels for 10%

profile of v2, /device:TPU:1, one launch (start us, length us, event | category | flops | bytes accessed | tf_op | source)
XLA Modules:
  0.0 97.2 jit_solution(12132735281485929197)
XLA Ops:
  0.0 0.0 copy-start.5
  0.0 0.0 copy-start.6
  0.0 0.0 copy-start
  0.0 1.1 %copy-done = f32[2,2,2,8,16,128]{5,4,3,2,1,0:T(8,128)S(1)} copy-done((f32[2,2,2,8,16,128]{5,4,3,2,1,0:T(8,128)S(1)}, f32[2,2,2,8,16,128]{5,4,3,2,1,0:T(8,128)}, u32[]{:S(2)}) %copy-start) | copy-done | bytes 524312
  1.1 0.0 copy-start.9
  1.1 0.0 copy-start.7
  1.1 1.4 %collective-permute-start.1 = (f32[8,1,16,128]{3,2,1,0:T(8,128)S(1)}, f32[8,1,16,128]{3,2,1,0:T(8,128)S(1)}, u32[]{:S(2)}, u32[]{:S(2)}) collective-permute-start(f32[8,1,16,128]{3,2,1,0:T(8,128)S(1)} %get-tuple-element.17), channel_id=1, source_target_pairs={{8,0},{16,8},{24,16},{32,24},{40,32},{48,40},{56,48},{64,56},{72,6... | collective-permute-start | bytes 196616 | tf_op jit(solution)/shard_map/ppermute | solution.py:359
  2.5 4.6 %collective-permute-start = (f32[8,2,16,128]{3,2,1,0:T(8,128)S(1)}, f32[8,2,16,128]{3,2,1,0:T(8,128)S(1)}, u32[]{:S(2)}, u32[]{:S(2)}) collective-permute-start(f32[8,2,16,128]{3,2,1,0:T(8,128)S(1)} %get-tuple-element.16), channel_id=1, source_target_pairs={{0,8},{8,16},{16,24},{24,32},{32,40},{40,48},{48,56},{56,64},{64,7... | collective-permute-start | bytes 393224 | tf_op jit(solution)/shard_map/ppermute | solution.py:359
  7.1 0.0 copy-done.9
  7.1 0.1 copy.9.win_ref
  7.3 0.0 copy-done.5
  7.3 0.0 copy-done.6
  7.3 0.0 copy-done.1
  7.3 0.0 copy-done.2
  7.3 0.0 copy-done.3
  7.3 0.0 copy-done.7
  7.3 7.1 %inner.1 = (bf16[128,64]{1,0:T(8,128)(2,1)S(1)}, f32[128,1]{1,0:T(8,128)S(1)}, bf16[2,128,128]{2,1,0:T(8,128)(2,1)S(1)}, f32[2,128,1]{2,1,0:T(8,128)S(1)}, bf16[...) custom-call(f32[8,8,16,128]{3,2,1,0:T(8,128)S(1)} %bitcast.9, ...), custom_call_target="tpu_custom_call" | custom-call | flops 7000000000 | bytes 1048576 | tf_op jit(solution)/shard_map/inner/pallas_call | solution.py:345
  14.5 0.0 copy-start.8
  14.5 0.0 collective-permute-done.1.xhi_ref
  14.5 0.0 collective-permute-done.xlo_ref
  14.5 0.1 send_y.1
  14.6 1.7 %copy-done.8 = f32[105,64,128]{2,1,0:T(8,128)} copy-done((f32[105,64,128]{2,1,0:T(8,128)}, f32[105,64,128]{2,1,0:T(8,128)S(1)}, u32[]{:S(2)}) %copy-start.8) | copy-done | bytes 3440664
  16.2 3.3 %collective-permute-start.3 = (f32[8,11,1,128]{3,2,1,0:T(1,128)S(1)}, f32[8,11,1,128]{3,2,1,0:T(1,128)S(1)}, u32[]{:S(2)}, u32[]{:S(2)}) collective-permute-start(f32[8,11,1,128]{3,2,1,0:T(1,128)S(1)} %get-tuple-element.19), channel_id=1, source_target_pairs={{1,0},{2,1},{3,2},{4,3},{5,4},{6,5},{7,6},{9,8},{10,9},{11,10},{12... | collective-permute-start | bytes 135176 | tf_op jit(solution)/shard_map/ppermute | solution.py:359
  19.5 3.5 %collective-permute-start.2 = (f32[8,11,2,128]{3,2,1,0:T(2,128)S(1)}, f32[8,11,2,128]{3,2,1,0:T(2,128)S(1)}, u32[]{:S(2)}, u32[]{:S(2)}) collective-permute-start(f32[8,11,2,128]{3,2,1,0:T(2,128)S(1)} %get-tuple-element.18), channel_id=1, source_target_pairs={{0,1},{1,2},{2,3},{3,4},{4,5},{5,6},{6,7},{8,9},{9,10},{10,11},{11... | collective-permute-start | bytes 270344 | tf_op jit(solution)/shard_map/ppermute | solution.py:359
  23.1 0.0 copy-start.4
  23.1 3.1 %side.1.side_ref = f32[45,64,128]{2,1,0:T(8,128)S(1)} custom-call(f32[8,8,16,128]{3,2,1,0:T(8,128)S(1)} %bitcast.11, f32[8,2,16,128]{3,2,1,0:T(8,128)S(1)} %collective-permute-done.xlo_ref, f32[8,1,16,128]{3,2,1,0:T(8,128)S(1)} %collective-permute-done.1.xhi_ref, bf16[128,64]{1,0:T(8,128)(2,1)S(1)} %get-tuple-element.20.w1_ref, ...), custom_call_target="tpu_custom_call" | custom-call | flops 4000000000 | bytes 1048576 | tf_op jit(solution)/shard_map/side/pallas_call | solution.py:345
  26.2 0.0 collective-permute-done.3.yhi_ref
  26.2 0.0 collective-permute-done.2.ylo_ref
  26.2 0.0 copy-done.4
  26.2 13.2 %stencils.1 = f32[6656,128]{1,0:T(8,128)S(1)} custom-call(s32[8,16]{1,0:T(8,128)S(1)} %copy-done.4, f32[8,8,16,128]{3,2,1,0:T(8,128)S(1)} %bitcast.12, f32[8,2,16,128]{3,2,1,0:T(8,128)S(1)} %collective-permute-done.xlo_ref, f32[8,1,16,128]{3,2,1,0:T(8,128)S(1)} %collective-permute-done.1.xhi_ref, f32[8,11,2,128]{3,2,1,0:T(2,128)S(1)} %collective-permute-done.2.ylo_ref, ...), custom_call_target="tpu_custom_call" | custom-call | flops 12000000000 | bytes 1048576 | tf_op jit(solution)/shard_map/stencils/pallas_call | solution.py:345
  39.4 55.5 %all_to_all.5 = f32[128,13,4,128]{3,2,1,0:T(4,128)S(1)} all-to-all(f32[128,13,4,128]{3,2,1,0:T(4,128)S(1)} %bitcast.7), channel_id=1, replica_groups=mesh['gx'=16,'gy'=8] {'gx','gy'}, dimensions={0} | all-to-all | bytes 6815744 | tf_op jit(solution)/shard_map/all_to_all | solution.py:387
  94.9 2.3 %unpack.1 = f32[27,256,128]{2,1,0:T(8,128)} custom-call(f32[6656,128]{1,0:T(8,128)S(1)} %bitcast.6), custom_call_target="tpu_custom_call" | custom-call | tf_op jit(solution)/shard_map/unpack/pallas_call | solution.py:388
  (4 shorter events, 0.0 us)
Async XLA Ops:
  0.0 7.3 %copy-start.5 = (f32[2,128]{1,0:T(2,128)S(1)}, f32[2,128]{1,0:T(2,128)}, u32[]{:S(2)}) copy-start(f32[2,128]{1,0:T(2,128)} %bmid_ref.1) | copy-start | bytes 3076
  0.0 7.3 %copy-start.6 = (f32[128]{0:T(128)S(1)}, f32[128]{0:T(128)}, u32[]{:S(2)}) copy-start(f32[128]{0:T(128)} %param.11) | copy-start | bytes 1540
  0.0 1.1 %copy-start = (f32[2,2,2,8,16,128]{5,4,3,2,1,0:T(8,128)S(1)}, f32[2,2,2,8,16,128]{5,4,3,2,1,0:T(8,128)}, u32[]{:S(2)}) copy-start(f32[2,2,2,8,16,128]{5,4,3,2,1,0:T(8,128)} %param.8) | copy-start | bytes 1572868
  1.1 6.1 %copy-start.9 = (bf16[128,27]{0,1:T(8,128)(2,1)S(1)}, bf16[128,27]{0,1:T(8,128)(2,1)}, u32[]{:S(2)}) copy-start(bf16[128,27]{0,1:T(8,128)(2,1)} %param.10) | copy-start | bytes 20740
  1.1 6.2 %copy-start.1 = (f32[2,2,2,8,16,128]{5,4,3,2,1,0:T(8,128)S(1)}, f32[2,2,2,8,16,128]{5,4,3,2,1,0:T(8,128)}, u32[]{:S(2)}) copy-start(f32[2,2,2,8,16,128]{5,4,3,2,1,0:T(8,128)} %param.8) | copy-start | bytes 1572868
  1.1 6.2 %copy-start.2 = (bf16[2,128,128]{2,1,0:T(8,128)(2,1)S(1)}, bf16[2,128,128]{2,1,0:T(8,128)(2,1)}, u32[]{:S(2)}) copy-start(bf16[2,128,128]{2,1,0:T(8,128)(2,1)} %wmid_ref.1) | copy-start | bytes 196612
  1.1 6.2 %copy-start.3 = (bf16[27,128]{1,0:T(8,128)(2,1)S(1)}, bf16[27,128]{1,0:T(8,128)(2,1)}, u32[]{:S(2)}) copy-start(bf16[27,128]{1,0:T(8,128)(2,1)} %wout_ref.1) | copy-start | bytes 20740
  1.1 6.2 %copy-start.7 = (f32[27]{0:T(128)S(1)}, f32[27]{0:T(128)}, u32[]{:S(2)}) copy-start(f32[27]{0:T(128)} %param.15) | copy-start | bytes 328
  1.1 13.3 %collective-permute-start.1 = (f32[8,1,16,128]{3,2,1,0:T(8,128)S(1)}, f32[8,1,16,128]{3,2,1,0:T(8,128)S(1)}, u32[]{:S(2)}, u32[]{:S(2)}) collective-permute-start(f32[8,1,16,128]{3,2,1,0:T(8,128)S(1)} %get-tuple-element.17), channel_id=1, source_target_pairs={{8,0},{16,8},{24,16},{32,24},{40,32},{48,40},{56,48},{64,56},{72,6... | collective-permute-start | bytes 196616 | tf_op jit(solution)/shard_map/ppermute | solution.py:359
  2.5 11.9 %collective-permute-start = (f32[8,2,16,128]{3,2,1,0:T(8,128)S(1)}, f32[8,2,16,128]{3,2,1,0:T(8,128)S(1)}, u32[]{:S(2)}, u32[]{:S(2)}) collective-permute-start(f32[8,2,16,128]{3,2,1,0:T(8,128)S(1)} %get-tuple-element.16), channel_id=1, source_target_pairs={{0,8},{8,16},{16,24},{24,32},{32,40},{40,48},{48,56},{56,64},{64,7... | collective-permute-start | bytes 393224 | tf_op jit(solution)/shard_map/ppermute | solution.py:359
  14.5 1.8 %copy-start.8 = (f32[105,64,128]{2,1,0:T(8,128)}, f32[105,64,128]{2,1,0:T(8,128)S(1)}, u32[]{:S(2)}) copy-start(f32[105,64,128]{2,1,0:T(8,128)S(1)} %get-tuple-element.26.inner_ref) | copy-start | bytes 10321924
  16.2 9.9 %collective-permute-start.3 = (f32[8,11,1,128]{3,2,1,0:T(1,128)S(1)}, f32[8,11,1,128]{3,2,1,0:T(1,128)S(1)}, u32[]{:S(2)}, u32[]{:S(2)}) collective-permute-start(f32[8,11,1,128]{3,2,1,0:T(1,128)S(1)} %get-tuple-element.19), channel_id=1, source_target_pairs={{1,0},{2,1},{3,2},{4,3},{5,4},{6,5},{7,6},{9,8},{10,9},{11,10},{12... | collective-permute-start | bytes 135176 | tf_op jit(solution)/shard_map/ppermute | solution.py:359
  19.5 6.7 %collective-permute-start.2 = (f32[8,11,2,128]{3,2,1,0:T(2,128)S(1)}, f32[8,11,2,128]{3,2,1,0:T(2,128)S(1)}, u32[]{:S(2)}, u32[]{:S(2)}) collective-permute-start(f32[8,11,2,128]{3,2,1,0:T(2,128)S(1)} %get-tuple-element.18), channel_id=1, source_target_pairs={{0,1},{1,2},{2,3},{3,4},{4,5},{5,6},{6,7},{8,9},{9,10},{10,11},{11... | collective-permute-start | bytes 270344 | tf_op jit(solution)/shard_map/ppermute | solution.py:359
  23.1 3.1 %copy-start.4 = (s32[8,16]{1,0:T(8,128)S(1)}, s32[8,16]{1,0:T(8,128)}, u32[]{:S(2)}) copy-start(s32[8,16]{1,0:T(8,128)} %owner_ref.1) | copy-start | bytes 1540

commit v3 on v2

--- a/solution.py
+++ b/solution.py
@@ -11,15 +11,12 @@
 SENT = [o for o in OFFSETS if o != (0, 0, -1)]
 PITCH = len(SENT)
 YP = 32
+UP = 24
 Y0 = 8
 
 
 def parity(o):
     return 4 * (o[0] != 0) + 2 * (o[1] != 0) + (o[2] != 0)
-
-
-def tile_row(o):
-    return 32 * (o[0] == -1) + 16 * (o[1] == -1) + 8 * (o[2] == -1) + parity(o)
 
 
 def offset_of_row(shape, dim):
@@ -86,7 +83,7 @@
     half = jnp.bfloat16(0.5)
     eye = lax.broadcasted_iota(jnp.int32, (128, 128), 0) == lax.broadcasted_iota(jnp.int32, (128, 128), 1)
     into = offset_of_row((27, 64), 1) == lax.broadcasted_iota(jnp.int32, (27, 64), 0)
-    out_of = offset_of_row((64, 27), 0) == lax.broadcasted_iota(jnp.int32, (64, 27), 1)
+    out_of = lax.broadcasted_iota(jnp.int32, (32, 27), 0) == lax.broadcasted_iota(jnp.int32, (32, 27), 1)
     ones = lambda m: jnp.where(m, 1.0, 0.0).astype(jnp.bfloat16)
     w1_ref[...] = jnp.dot(win_ref[...] * half, ones(into), preferred_element_type=jnp.float32).astype(jnp.bfloat16)
     wo_ref[...] = jnp.dot(ones(out_of), wout_ref[...] * half, preferred_element_type=jnp.float32).astype(jnp.bfloat16)
@@ -142,13 +139,13 @@
 
 def main_kernel(nx, ny, owner_ref, coef_ref, xlo_ref, xhi_ref, ylo_ref, yhi_ref,
                 w1_ref, b1_ref, wm_ref, bm_ref, wo_ref, bo_ref, inner_ref, side_ref, out_ref,
-                k_ref, r_ref, f_ref, rt_ref, t_ref, u_ref, s_ref, count_ref):
+                k_ref, r_ref, f_ref, t_ref, u_ref, s_ref, count_ref):
     nz = 128
     layers = (w1_ref, b1_ref, wm_ref, bm_ref, wo_ref, bo_ref)
     ex, ey = nx + 3, ny + 3
     hx, hy = nx + 2, ny + 2
     kp = ex * YP
-    up = hx * hy
+    up = hx * UP
     last_x = lax.axis_index("gx") == lax.axis_size("gx") - 1
     last_y = lax.axis_index("gy") == lax.axis_size("gy") - 1
 
@@ -160,25 +157,29 @@
             k_ref[p, x, Y0 - 2:Y0] = ylo_ref[p, x]
             k_ref[p, x, Y0 + ny:Y0 + ny + 1] = yhi_ref[p, x]
     flat_k = k_ref.reshape(8 * kp, nz)
-    flat_r = r_ref.reshape(8 * kp, nz)
-
-    def roots(i, _):
-        rows = pl.ds(pl.multiple_of(i * YP, YP), YP)
-        flat_r[rows, :] = jnp.sqrt(flat_k[rows, :])
-        return _
-
-    lax.fori_loop(0, 8 * ex, roots, 0)
+    flat_r = r_ref.reshape(12 * kp, nz)
+
+    def inverse_root(v):
+        return lax.rsqrt(jnp.maximum(v, 1e-30))
+
+    def roots(x, _):
+        for p in range(8):
+            for b in range(0, YP, 8):
+                rows = pl.ds(pl.multiple_of(p * kp + x * YP + b, 8), 8)
+                v = flat_k[rows, :]
+                v = v * inverse_root(v)
+                flat_r[rows, :] = v
+                if p % 2:
+                    flat_r[pl.ds(pl.multiple_of((8 + p // 2) * kp + x * YP + b, 8), 8), :] = z_before(v)
+        return _
+
+    lax.fori_loop(0, ex, roots, 0)
 
     rim = {0: 0, 1: 1, 2: 2, ey - 2: 3, ey - 1: 4}
 
     def tiles(x, _):
-        for y in range(ey):
-            at = pl.ds(x * YP + Y0 - 2 + y, 8, stride=kp)
-            if y in rim:
-                f_ref[x, rim[y]] = feature_tile(flat_k[at, :])
-            rt = flat_r[at, :]
-            rt_ref[x, y, 0:8] = rt
-            rt_ref[x, y, 8:16] = z_before(rt)
+        for y, at in rim.items():
+            f_ref[x, at] = feature_tile(flat_k[pl.ds(x * YP + Y0 - 2 + y, 8, stride=kp), :])
         return _
 
     lax.fori_loop(0, ex, tiles, 0)
@@ -193,12 +194,12 @@
 
             for p in range(8):
                 px, py, pz = p >> 2, (p >> 1) & 1, p & 1
-                own = at(px, py, pz, 0, 0)
+                own = flat_k[pl.ds(p * kp + (x + 1) * YP + Y0 - 1 + blk, rows), :]
                 total = at(1 - px, py, pz, 0, 0) + at(1 - px, py, pz, 1 if px else -1, 0)
                 total += at(px, 1 - py, pz, 0, 0) + at(px, 1 - py, pz, 0, 1 if py else -1)
                 beside = at(px, py, 1 - pz, 0, 0)
                 total += beside + (z_after(beside) if pz else z_before(beside))
-                t = jnp.where(own > 0.0, total / jnp.where(own > 0.0, own, 1.0), 0.0)
+                t = total * inverse_root(own)
                 t_ref[p, x, pl.ds(blk, rows), :] = t
                 if pz:
                     t_ref[8 + p // 2, x, pl.ds(blk, rows), :] = z_before(t)
@@ -207,15 +208,9 @@
     lax.fori_loop(0, nx + 1, ratios, 0)
 
     def put(x, y, wy):
-        for q, (sx, sy) in enumerate(((0, 0), (0, 1), (1, 0), (1, 1))):
-            for sz in range(2):
-                part = 16 * q + 8 * sz
-                u = wy[part:part + 8] * rt_ref[x + 1 - sx, y + 1 - sy, 8 * sz:8 * sz + 8]
-                at = part * up + x * hy + y
-                u_ref[0, pl.ds(at, 8, stride=up), :] = u
-                u_ref[1, pl.ds(at, 8, stride=up), :] = z_after(u)
-                if not sz:
-                    u_ref[2, pl.ds(at, 8, stride=up), :] = z_before(u)
+        for n in range(0, 27, 8):
+            size = min(8, 27 - n)
+            u_ref[0, pl.ds(n * up + x * UP + y, size, stride=up), :] = wy[n:n + size]
 
     def put_inner(x, _):
         for y in range(1, ny):
@@ -225,29 +220,42 @@
     lax.fori_loop(1, nx, put_inner, 0)
 
     def put_side(i, _):
-        keep = jnp.where(jnp.logical_and(i == 2, last_x), 0.0, 1.0)
         for y in range(1, ny):
-            put(jnp.where(i == 2, hx - 1, i), y + 1, side_ref[i * (ny - 1) + y - 1] * keep)
+            put(jnp.where(i == 2, hx - 1, i), y + 1, side_ref[i * (ny - 1) + y - 1])
         return _
 
     lax.fori_loop(0, 3, put_side, 0)
     columns = [(x, y) for y in (0, 1, hy - 1) for x in range(hx)]
     w = mlp(lambda x, y: f_ref[x, rim[y]], [(x + 1, y + 1) for x, y in columns], layers)
     for n, (x, y) in enumerate(columns):
-        wy = w[:, n * nz:(n + 1) * nz]
-        if x == hx - 1:
-            wy = wy * jnp.where(last_x, 0.0, 1.0)
-        if y == hy - 1:
-            wy = wy * jnp.where(last_y, 0.0, 1.0)
-        put(x, y, wy)
+        put(x, y, w[:, n * nz:(n + 1) * nz])
+
+    def scale(x, _):
+        past_x = jnp.logical_and(last_x, x == hx - 1)
+        for b in range(0, UP, 8):
+            y = lax.broadcasted_iota(jnp.int32, (8, nz), 0) + b
+            past = jnp.logical_or(past_x, jnp.logical_and(last_y, y == hy - 1))
+            for n, o in enumerate(OFFSETS):
+                rows = pl.ds(pl.multiple_of(n * up + x * UP + b, 8), 8)
+                plane = 8 + parity(o) // 2 if o[2] == -1 else parity(o)
+                r = flat_r[pl.ds(plane * kp + (x + 1 - (o[0] == -1)) * YP + Y0 - 1 + b - (o[1] == -1), 8), :]
+                u = jnp.where(past, 0.0, u_ref[0, rows, :] * r)
+                u_ref[0, rows, :] = u
+                if o[2] != 1:
+                    u_ref[1, rows, :] = z_after(u)
+                if o[2] != -1:
+                    u_ref[2, rows, :] = z_before(u)
+        return _
+
+    lax.fori_loop(0, hx, scale, 0)
 
     def galerkin(x, _):
         for yb in range(0, ny, 8):
 
             def u_at(f, o):
-                plane = tile_row(f)
+                plane = OFFSETS.index(f)
                 which = {0: 0, 1: 1, -1: 2}[o[2]]
-                row = plane * up + (x + 1 + o[0]) * hy + yb + 1 + o[1]
+                row = plane * up + (x + 1 + o[0]) * UP + yb + 1 + o[1]
                 return u_ref[which, pl.ds(row, 8), :]
 
             own = {f: u_at(f, (0, 0, 0)) for f in OFFSETS}
@@ -341,7 +349,7 @@
     f32 = lambda *shape: jax.ShapeDtypeStruct(shape, jnp.float32)
     bf16 = lambda *shape: jax.ShapeDtypeStruct(shape, jnp.bfloat16)
 
-    def call(kernel, name, out_shape, args, scratch=(), limit=48, us=1, first=vmem):
+    def call(kernel, name, out_shape, args, scratch=(), limit=32, us=1, first=vmem):
         return pl.pallas_call(
             kernel,
             out_shape=out_shape,
@@ -364,23 +372,22 @@
     ylo, yhi = send(up, "gy", 1), send(down, "gy", -1)
     *layers, inner = call(
         functools.partial(inner_kernel, nx, ny), "inner",
-        (bf16(128, 64), f32(128, 1), bf16(2, 128, 128), f32(2, 128, 1), bf16(64, 128), f32(64, 1),
-         f32((nx - 1) * (ny - 1), 64, nz)),
+        (bf16(128, 64), f32(128, 1), bf16(2, 128, 128), f32(2, 128, 1), bf16(32, 128), f32(32, 1),
+         f32((nx - 1) * (ny - 1), 32, nz)),
         (k, w_in, b_in[None], w_mid, b_mid, w_out, b_out[None]),
         scratch=[pltpu.VMEM((nx, ny, 16, nz), jnp.bfloat16)], us=7)
     side = call(
-        functools.partial(side_kernel, nx, ny), "side", f32(3 * (ny - 1), 64, nz), (k, xlo, xhi, *layers),
+        functools.partial(side_kernel, nx, ny), "side", f32(3 * (ny - 1), 32, nz), (k, xlo, xhi, *layers),
         scratch=[pltpu.VMEM((8, 5, ny, nz), jnp.float32), pltpu.VMEM((5, ny, 16, nz), jnp.bfloat16)], us=4)
     out = call(
         functools.partial(main_kernel, nx, ny), "stencils", f32(devices * 2 * PITCH, nz),
         (owner, k, xlo, xhi, ylo, yhi, *layers, inner, side), us=12, first=smem,
         scratch=[
             pltpu.VMEM((8, ex, YP, nz), jnp.float32),
-            pltpu.VMEM((8, ex, YP, nz), jnp.float32),
+            pltpu.VMEM((12, ex, YP, nz), jnp.float32),
             pltpu.VMEM((ex, 5, 16, nz), jnp.bfloat16),
-            pltpu.VMEM((ex, ey, 16, nz), jnp.float32),
             pltpu.VMEM((12, nx + 1, 24, nz), jnp.float32),
-            pltpu.VMEM((3, 64 * hx * hy, nz), jnp.float32),
+            pltpu.VMEM((3, 27 * hx * UP, nz), jnp.float32),
             pltpu.VMEM((PITCH * nx * ny, nz), jnp.float32),
             pltpu.SMEM((devices,), jnp.int32),
         ])

time: 97.5 us -> 93.9 us (0.963)
  Pallas kernels: 25.7 us -> 23.8 us
  local copies, waits for them, and re-layouts: 2.89 us -> 1.23 us
    pallas_call x5, Pallas kernels: 23.5 us -> 21.6 us  [call(): pl.pallas_call(kernel, out_shape=out_shape, in_specs=[first] + [vmem] * (...]
    unnamed x21 -> x19, local copies, waits for them, and re-layouts: 2.89 us -> 1.23 us
  transfers between devices with their start and end apart: 4 -> 4, of which waited for: 0 -> 0; matrix products, arithmetic and copies ran while one was open for 0% -> 0% of each run, Pallas kernels for 10% -> 11%
where the time goes in v3:
time: 93.9 us; the launch traced here: 93.6 us
  blocking collectives  55.5 us (59%)
  Pallas kernels  23.8 us (25%)
  starting transfers between devices  12.8 us (14%)
  local copies, waits for them, and re-layouts  1.23 us (1%)
    all_to_all x1, blocking collectives, per_device(): lax.all_to_all(out.reshape(devices, -1, 4, nz), ('gx', 'gy'), split_axis=...  55.5 us
    pallas_call x5, Pallas kernels, call(): pl.pallas_call(kernel, out_shape=out_shape, in_specs=[first] + [vmem] * (...  21.6 us
    ppermute x4, starting transfers between devices, send(): return lax.ppermute(v, axis, pairs)  12.8 us
    pallas_call x1, Pallas kernels, per_device(): pl.pallas_call(unpack_kernel, grid=(3,), out_shape=f32(27, devices * 2, n...  2.28 us
  transfers between devices with their start and end apart: 4, of which 0 were waited for; matrix products, arithmetic and copies ran while one was open for 0% of the time, Pallas kernels for 11%

profile of v3, /device:TPU:1, one launch (start us, length us, event | category | flops | bytes accessed | tf_op | source)
XLA Modules:
  0.0 93.6 jit_solution(10820427367968881018)
XLA Ops:
  0.0 0.0 copy-start.5
  0.0 0.0 copy-start.6
  0.0 0.0 copy-start
  0.0 1.1 %copy-done = f32[2,2,2,8,16,128]{5,4,3,2,1,0:T(8,128)S(1)} copy-done((f32[2,2,2,8,16,128]{5,4,3,2,1,0:T(8,128)S(1)}, f32[2,2,2,8,16,128]{5,4,3,2,1,0:T(8,128)}, u32[]{:S(2)}) %copy-start) | copy-done | bytes 524312
  1.1 0.0 copy-start.8
  1.1 0.0 copy-start.1
  1.1 0.0 copy-start.2
  1.1 0.0 copy-start.7
  1.1 1.4 %collective-permute-start.1 = (f32[8,1,16,128]{3,2,1,0:T(8,128)S(1)}, f32[8,1,16,128]{3,2,1,0:T(8,128)S(1)}, u32[]{:S(2)}, u32[]{:S(2)}) collective-permute-start(f32[8,1,16,128]{3,2,1,0:T(8,128)S(1)} %get-tuple-element.17), channel_id=1, source_target_pairs={{8,0},{16,8},{24,16},{32,24},{40,32},{48,40},{56,48},{64,56},{72,6... | collective-permute-start | bytes 196616 | tf_op jit(solution)/shard_map/ppermute | solution.py:367
  2.5 4.6 %collective-permute-start = (f32[8,2,16,128]{3,2,1,0:T(8,128)S(1)}, f32[8,2,16,128]{3,2,1,0:T(8,128)S(1)}, u32[]{:S(2)}, u32[]{:S(2)}) collective-permute-start(f32[8,2,16,128]{3,2,1,0:T(8,128)S(1)} %get-tuple-element.16), channel_id=1, source_target_pairs={{0,8},{8,16},{16,24},{24,32},{32,40},{40,48},{48,56},{56,64},{64,7... | collective-permute-start | bytes 393224 | tf_op jit(solution)/shard_map/ppermute | solution.py:367
  7.1 0.0 copy-done.8
  7.1 0.1 copy.9.win_ref
  7.3 0.0 copy-done.5
  7.3 0.0 copy-done.6
  7.3 0.0 copy-done.1
  7.3 0.0 copy-done.2
  7.3 0.0 copy-done.3
  7.3 0.0 copy-done.7
  7.3 7.0 %inner.1 = (bf16[128,64]{1,0:T(8,128)(2,1)S(1)}, f32[128,1]{1,0:T(8,128)S(1)}, bf16[2,128,128]{2,1,0:T(8,128)(2,1)S(1)}, f32[2,128,1]{2,1,0:T(8,128)S(1)}, bf16[...) custom-call(f32[8,8,16,128]{3,2,1,0:T(8,128)S(1)} %bitcast.9, ...), custom_call_target="tpu_custom_call" | custom-call | flops 7000000000 | bytes 1048576 | tf_op jit(solution)/shard_map/inner/pallas_call | solution.py:353
  14.4 0.0 collective-permute-done.1.xhi_ref
  14.4 0.0 collective-permute-done.xlo_ref
  14.4 0.1 send_y.1
  14.5 3.3 %collective-permute-start.3 = (f32[8,11,1,128]{3,2,1,0:T(1,128)S(1)}, f32[8,11,1,128]{3,2,1,0:T(1,128)S(1)}, u32[]{:S(2)}, u32[]{:S(2)}) collective-permute-start(f32[8,11,1,128]{3,2,1,0:T(1,128)S(1)} %get-tuple-element.19), channel_id=1, source_target_pairs={{1,0},{2,1},{3,2},{4,3},{5,4},{6,5},{7,6},{9,8},{10,9},{11,10},{12... | collective-permute-start | bytes 135176 | tf_op jit(solution)/shard_map/ppermute | solution.py:367
  17.8 3.5 %collective-permute-start.2 = (f32[8,11,2,128]{3,2,1,0:T(2,128)S(1)}, f32[8,11,2,128]{3,2,1,0:T(2,128)S(1)}, u32[]{:S(2)}, u32[]{:S(2)}) collective-permute-start(f32[8,11,2,128]{3,2,1,0:T(2,128)S(1)} %get-tuple-element.18), channel_id=1, source_target_pairs={{0,1},{1,2},{2,3},{3,4},{4,5},{5,6},{6,7},{8,9},{9,10},{10,11},{11... | collective-permute-start | bytes 270344 | tf_op jit(solution)/shard_map/ppermute | solution.py:367
  21.3 0.0 copy-start.4
  21.3 3.1 %side.1.side_ref = f32[45,32,128]{2,1,0:T(8,128)S(1)} custom-call(f32[8,8,16,128]{3,2,1,0:T(8,128)S(1)} %bitcast.11, f32[8,2,16,128]{3,2,1,0:T(8,128)S(1)} %collective-permute-done.xlo_ref, f32[8,1,16,128]{3,2,1,0:T(8,128)S(1)} %collective-permute-done.1.xhi_ref, bf16[128,64]{1,0:T(8,128)(2,1)S(1)} %get-tuple-element.20.w1_ref, ...), custom_call_target="tpu_custom_call" | custom-call | flops 4000000000 | bytes 1048576 | tf_op jit(solution)/shard_map/side/pallas_call | solution.py:353
  24.4 0.0 collective-permute-done.3.yhi_ref
  24.4 0.0 collective-permute-done.2.ylo_ref
  24.4 0.0 copy-done.4
  24.4 11.4 %stencils.1 = f32[6656,128]{1,0:T(8,128)S(1)} custom-call(s32[8,16]{1,0:T(8,128)S(1)} %copy-done.4, f32[8,8,16,128]{3,2,1,0:T(8,128)S(1)} %bitcast.12, f32[8,2,16,128]{3,2,1,0:T(8,128)S(1)} %collective-permute-done.xlo_ref, f32[8,1,16,128]{3,2,1,0:T(8,128)S(1)} %collective-permute-done.1.xhi_ref, f32[8,11,2,128]{3,2,1,0:T(2,128)S(1)} %collective-permute-done.2.ylo_ref, ...), custom_call_target="tpu_custom_call" | custom-call | flops 12000000000 | bytes 1048576 | tf_op jit(solution)/shard_map/stencils/pallas_call | solution.py:353
  35.8 55.5 %all_to_all.5 = f32[128,13,4,128]{3,2,1,0:T(4,128)S(1)} all-to-all(f32[128,13,4,128]{3,2,1,0:T(4,128)S(1)} %bitcast.7), channel_id=1, replica_groups=mesh['gx'=16,'gy'=8] {'gx','gy'}, dimensions={0} | all-to-all | bytes 6815744 | tf_op jit(solution)/shard_map/all_to_all | solution.py:394
  91.3 2.3 %unpack.1 = f32[27,256,128]{2,1,0:T(8,128)} custom-call(f32[6656,128]{1,0:T(8,128)S(1)} %bitcast.6), custom_call_target="tpu_custom_call" | custom-call | tf_op jit(solution)/shard_map/unpack/pallas_call | solution.py:395
  (2 shorter events, 0.0 us)
Async XLA Ops:
  0.0 7.3 %copy-start.5 = (f32[2,128]{1,0:T(2,128)S(1)}, f32[2,128]{1,0:T(2,128)}, u32[]{:S(2)}) copy-start(f32[2,128]{1,0:T(2,128)} %bmid_ref.1) | copy-start | bytes 3076
  0.0 7.3 %copy-start.6 = (f32[128]{0:T(128)S(1)}, f32[128]{0:T(128)}, u32[]{:S(2)}) copy-start(f32[128]{0:T(128)} %param.11) | copy-start | bytes 1540
  0.0 1.1 %copy-start = (f32[2,2,2,8,16,128]{5,4,3,2,1,0:T(8,128)S(1)}, f32[2,2,2,8,16,128]{5,4,3,2,1,0:T(8,128)}, u32[]{:S(2)}) copy-start(f32[2,2,2,8,16,128]{5,4,3,2,1,0:T(8,128)} %param.8) | copy-start | bytes 1572868
  1.1 6.1 %copy-start.8 = (bf16[128,27]{0,1:T(8,128)(2,1)S(1)}, bf16[128,27]{0,1:T(8,128)(2,1)}, u32[]{:S(2)}) copy-start(bf16[128,27]{0,1:T(8,128)(2,1)} %param.10) | copy-start | bytes 20740
  1.1 6.2 %copy-start.1 = (f32[2,2,2,8,16,128]{5,4,3,2,1,0:T(8,128)S(1)}, f32[2,2,2,8,16,128]{5,4,3,2,1,0:T(8,128)}, u32[]{:S(2)}) copy-start(f32[2,2,2,8,16,128]{5,4,3,2,1,0:T(8,128)} %param.8) | copy-start | bytes 1572868
  1.1 6.2 %copy-start.2 = (bf16[2,128,128]{2,1,0:T(8,128)(2,1)S(1)}, bf16[2,128,128]{2,1,0:T(8,128)(2,1)}, u32[]{:S(2)}) copy-start(bf16[2,128,128]{2,1,0:T(8,128)(2,1)} %wmid_ref.1) | copy-start | bytes 196612
  1.1 6.2 %copy-start.3 = (bf16[27,128]{1,0:T(8,128)(2,1)S(1)}, bf16[27,128]{1,0:T(8,128)(2,1)}, u32[]{:S(2)}) copy-start(bf16[27,128]{1,0:T(8,128)(2,1)} %wout_ref.1) | copy-start | bytes 20740
  1.1 6.2 %copy-start.7 = (f32[27]{0:T(128)S(1)}, f32[27]{0:T(128)}, u32[]{:S(2)}) copy-start(f32[27]{0:T(128)} %param.15) | copy-start | bytes 328
  1.1 13.3 %collective-permute-start.1 = (f32[8,1,16,128]{3,2,1,0:T(8,128)S(1)}, f32[8,1,16,128]{3,2,1,0:T(8,128)S(1)}, u32[]{:S(2)}, u32[]{:S(2)}) collective-permute-start(f32[8,1,16,128]{3,2,1,0:T(8,128)S(1)} %get-tuple-element.17), channel_id=1, source_target_pairs={{8,0},{16,8},{24,16},{32,24},{40,32},{48,40},{56,48},{64,56},{72,6... | collective-permute-start | bytes 196616 | tf_op jit(solution)/shard_map/ppermute | solution.py:367
  2.5 11.8 %collective-permute-start = (f32[8,2,16,128]{3,2,1,0:T(8,128)S(1)}, f32[8,2,16,128]{3,2,1,0:T(8,128)S(1)}, u32[]{:S(2)}, u32[]{:S(2)}) collective-permute-start(f32[8,2,16,128]{3,2,1,0:T(8,128)S(1)} %get-tuple-element.16), channel_id=1, source_target_pairs={{0,8},{8,16},{16,24},{24,32},{32,40},{40,48},{48,56},{56,64},{64,7... | collective-permute-start | bytes 393224 | tf_op jit(solution)/shard_map/ppermute | solution.py:367
  14.5 9.9 %collective-permute-start.3 = (f32[8,11,1,128]{3,2,1,0:T(1,128)S(1)}, f32[8,11,1,128]{3,2,1,0:T(1,128)S(1)}, u32[]{:S(2)}, u32[]{:S(2)}) collective-permute-start(f32[8,11,1,128]{3,2,1,0:T(1,128)S(1)} %get-tuple-element.19), channel_id=1, source_target_pairs={{1,0},{2,1},{3,2},{4,3},{5,4},{6,5},{7,6},{9,8},{10,9},{11,10},{12... | collective-permute-start | bytes 135176 | tf_op jit(solution)/shard_map/ppermute | solution.py:367
  17.8 6.6 %collective-permute-start.2 = (f32[8,11,2,128]{3,2,1,0:T(2,128)S(1)}, f32[8,11,2,128]{3,2,1,0:T(2,128)S(1)}, u32[]{:S(2)}, u32[]{:S(2)}) collective-permute-start(f32[8,11,2,128]{3,2,1,0:T(2,128)S(1)} %get-tuple-element.18), channel_id=1, source_target_pairs={{0,1},{1,2},{2,3},{3,4},{4,5},{5,6},{6,7},{8,9},{9,10},{10,11},{11... | collective-permute-start | bytes 270344 | tf_op jit(solution)/shard_map/ppermute | solution.py:367
  21.3 3.1 %copy-start.4 = (s32[8,16]{1,0:T(8,128)S(1)}, s32[8,16]{1,0:T(8,128)}, u32[]{:S(2)}) copy-start(s32[8,16]{1,0:T(8,128)} %owner_ref.1) | copy-start | bytes 1540

commit v4 on v3

--- a/solution.py
+++ b/solution.py
@@ -10,9 +10,7 @@
 OFFSETS = [(a, b, c) for a in (-1, 0, 1) for b in (-1, 0, 1) for c in (-1, 0, 1)]
 SENT = [o for o in OFFSETS if o != (0, 0, -1)]
 PITCH = len(SENT)
-YP = 32
-UP = 24
-Y0 = 8
+YP = 24
 
 
 def parity(o):
@@ -95,15 +93,16 @@
     layers = (w1_ref, b1_ref, wm_ref, bm_ref, wo_ref, bo_ref)
     flat = k_ref.reshape(8 * nx * ny, nz)
 
-    def tiles(x, _):
+    def tiles(x):
         for y in range(ny):
             f_ref[x, y] = feature_tile(flat[pl.ds(x * ny + y, 8, stride=nx * ny), :])
-        return _
-
-    lax.fori_loop(0, nx, tiles, 0)
+
+    tiles(0)
+    tiles(1)
 
     def row(x, _):
         w = mlp(lambda a, b: f_ref[a, b], [(x, y) for y in range(1, ny)], layers)
+        tiles(jnp.minimum(x + 1, nx - 1))
         for y in range(1, ny):
             w_ref[(x - 1) * (ny - 1) + y - 1] = w[:, (y - 1) * nz:y * nz]
         return _
@@ -139,78 +138,69 @@
 
 def main_kernel(nx, ny, owner_ref, coef_ref, xlo_ref, xhi_ref, ylo_ref, yhi_ref,
                 w1_ref, b1_ref, wm_ref, bm_ref, wo_ref, bo_ref, inner_ref, side_ref, out_ref,
-                k_ref, r_ref, f_ref, t_ref, u_ref, s_ref, count_ref):
+                k_ref, r_ref, f_ref, t_ref, u_ref, keep_ref, s_ref, slot_ref, count_ref):
     nz = 128
     layers = (w1_ref, b1_ref, wm_ref, bm_ref, wo_ref, bo_ref)
     ex, ey = nx + 3, ny + 3
     hx, hy = nx + 2, ny + 2
-    kp = ex * YP
-    up = hx * UP
+    kp = r_ref.shape[0] // 12
+    tp = t_ref.shape[0] // 12
+    up = (hx + 1) * YP
     last_x = lax.axis_index("gx") == lax.axis_size("gx") - 1
     last_y = lax.axis_index("gy") == lax.axis_size("gy") - 1
 
     for p in range(8):
-        k_ref[p, 2:2 + nx, Y0:Y0 + ny] = coef_ref[p]
-        k_ref[p, 0:2, Y0:Y0 + ny] = xlo_ref[p]
-        k_ref[p, 2 + nx:, Y0:Y0 + ny] = xhi_ref[p]
         for x in range(ex):
-            k_ref[p, x, Y0 - 2:Y0] = ylo_ref[p, x]
-            k_ref[p, x, Y0 + ny:Y0 + ny + 1] = yhi_ref[p, x]
-    flat_k = k_ref.reshape(8 * kp, nz)
-    flat_r = r_ref.reshape(12 * kp, nz)
+            row = p * kp + (x + 1) * YP
+            if x < 2:
+                own = xlo_ref[p, x]
+            elif x < 2 + nx:
+                own = coef_ref[p, x - 2]
+            else:
+                own = xhi_ref[p, x - 2 - nx]
+            k_ref[row - 2:row] = ylo_ref[p, x]
+            k_ref[row:row + ny] = own
+            k_ref[row + ny:row + ny + 1] = yhi_ref[p, x]
 
     def inverse_root(v):
         return lax.rsqrt(jnp.maximum(v, 1e-30))
 
-    def roots(x, _):
+    def roots(i, _):
         for p in range(8):
-            for b in range(0, YP, 8):
-                rows = pl.ds(pl.multiple_of(p * kp + x * YP + b, 8), 8)
-                v = flat_k[rows, :]
-                v = v * inverse_root(v)
-                flat_r[rows, :] = v
-                if p % 2:
-                    flat_r[pl.ds(pl.multiple_of((8 + p // 2) * kp + x * YP + b, 8), 8), :] = z_before(v)
-        return _
-
-    lax.fori_loop(0, ex, roots, 0)
-
-    rim = {0: 0, 1: 1, 2: 2, ey - 2: 3, ey - 1: 4}
-
-    def tiles(x, _):
-        for y, at in rim.items():
-            f_ref[x, at] = feature_tile(flat_k[pl.ds(x * YP + Y0 - 2 + y, 8, stride=kp), :])
-        return _
-
-    lax.fori_loop(0, ex, tiles, 0)
-
-    def ratios(x, _):
-        for blk in range(0, ny + 1, 8):
-            rows = min(8, ny + 1 - blk)
-
-            def at(px, py, pz, dx, dy):
-                p = 4 * px + 2 * py + pz
-                return flat_r[pl.ds(p * kp + (x + 1 + dx) * YP + Y0 - 1 + blk + dy, rows), :]
-
-            for p in range(8):
-                px, py, pz = p >> 2, (p >> 1) & 1, p & 1
-                own = flat_k[pl.ds(p * kp + (x + 1) * YP + Y0 - 1 + blk, rows), :]
-                total = at(1 - px, py, pz, 0, 0) + at(1 - px, py, pz, 1 if px else -1, 0)
-                total += at(px, 1 - py, pz, 0, 0) + at(px, 1 - py, pz, 0, 1 if py else -1)
-                beside = at(px, py, 1 - pz, 0, 0)
-                total += beside + (z_after(beside) if pz else z_before(beside))
-                t = total * inverse_root(own)
-                t_ref[p, x, pl.ds(blk, rows), :] = t
-                if pz:
-                    t_ref[8 + p // 2, x, pl.ds(blk, rows), :] = z_before(t)
-        return _
-
-    lax.fori_loop(0, nx + 1, ratios, 0)
+            rows = pl.ds(pl.multiple_of(p * kp + 8 * i, 8), 8)
+            v = k_ref[rows, :]
+            v = v * inverse_root(v)
+            r_ref[rows, :] = v
+            if p % 2:
+                r_ref[pl.ds(pl.multiple_of((8 + p // 2) * kp + 8 * i, 8), 8), :] = z_before(v)
+        return _
+
+    lax.fori_loop(0, kp // 8, roots, 0, unroll=6)
+
+    def ratios(i, _):
+        def at(px, py, pz, dx, dy):
+            p = 4 * px + 2 * py + pz
+            return r_ref[pl.ds(p * kp + 8 * i + YP + YP * dx + dy, 8), :]
+
+        for p in range(8):
+            px, py, pz = p >> 2, (p >> 1) & 1, p & 1
+            own = k_ref[pl.ds(pl.multiple_of(p * kp + 8 * i + YP, 8), 8), :]
+            total = at(1 - px, py, pz, 0, 0) + at(1 - px, py, pz, 1 if px else -1, 0)
+            total += at(px, 1 - py, pz, 0, 0) + at(px, 1 - py, pz, 0, 1 if py else -1)
+            beside = at(px, py, 1 - pz, 0, 0)
+            total += beside + (z_after(beside) if pz else z_before(beside))
+            t = total * inverse_root(own)
+            t_ref[pl.ds(pl.multiple_of(p * tp + 8 * i, 8), 8), :] = t
+            if pz:
+                t_ref[pl.ds(pl.multiple_of((8 + p // 2) * tp + 8 * i, 8), 8), :] = z_before(t)
+        return _
+
+    lax.fori_loop(0, tp // 8, ratios, 0, unroll=5)
 
     def put(x, y, wy):
         for n in range(0, 27, 8):
             size = min(8, 27 - n)
-            u_ref[0, pl.ds(n * up + x * UP + y, size, stride=up), :] = wy[n:n + size]
+            u_ref[0, pl.ds(n * up + (x + 1) * YP + y - 1, size, stride=up), :] = wy[n:n + size]
 
     def put_inner(x, _):
         for y in range(1, ny):
@@ -225,37 +215,65 @@
         return _
 
     lax.fori_loop(0, 3, put_side, 0)
+    rim = {0: 0, 1: 1, 2: 2, ey - 2: 3, ey - 1: 4}
+    for x in range(ex):
+        for y, at in rim.items():
+            f_ref[x, at] = feature_tile(k_ref[pl.ds((x + 1) * YP + y - 2, 8, stride=kp), :])
     columns = [(x, y) for y in (0, 1, hy - 1) for x in range(hx)]
     w = mlp(lambda x, y: f_ref[x, rim[y]], [(x + 1, y + 1) for x, y in columns], layers)
+    out_ref[...] = jnp.zeros(out_ref.shape, jnp.float32)
     for n, (x, y) in enumerate(columns):
         put(x, y, w[:, n * nz:(n + 1) * nz])
 
-    def scale(x, _):
-        past_x = jnp.logical_and(last_x, x == hx - 1)
-        for b in range(0, UP, 8):
-            y = lax.broadcasted_iota(jnp.int32, (8, nz), 0) + b
-            past = jnp.logical_or(past_x, jnp.logical_and(last_y, y == hy - 1))
-            for n, o in enumerate(OFFSETS):
-                rows = pl.ds(pl.multiple_of(n * up + x * UP + b, 8), 8)
-                plane = 8 + parity(o) // 2 if o[2] == -1 else parity(o)
-                r = flat_r[pl.ds(plane * kp + (x + 1 - (o[0] == -1)) * YP + Y0 - 1 + b - (o[1] == -1), 8), :]
-                u = jnp.where(past, 0.0, u_ref[0, rows, :] * r)
-                u_ref[0, rows, :] = u
-                if o[2] != 1:
-                    u_ref[1, rows, :] = z_after(u)
-                if o[2] != -1:
-                    u_ref[2, rows, :] = z_before(u)
-        return _
-
-    lax.fori_loop(0, hx, scale, 0)
+    row = lax.broadcasted_iota(jnp.int32, (up, nz), 0)
+    keep_ref[...] = jnp.where(jnp.logical_and(last_x, row >= hx * YP - 1), 0.0, 1.0)
+
+    @pl.when(last_y)
+    def _():
+        for x in range(hx):
+            keep_ref[(x + 1) * YP + ny:(x + 1) * YP + ny + 1] = jnp.zeros((1, nz), jnp.float32)
+
+    def scale(i, _):
+        keep = keep_ref[pl.ds(pl.multiple_of(8 * i, 8), 8), :]
+        rows = [pl.ds(pl.multiple_of(n * up + 8 * i, 8), 8) for n in range(27)]
+        scaled = []
+        for n, o in enumerate(OFFSETS):
+            plane = 8 + parity(o) // 2 if o[2] == -1 else parity(o)
+            at = plane * kp + 8 * i + (0 if o[0] == -1 else YP) + (-1 if o[1] == -1 else 0)
+            scaled.append(u_ref[0, rows[n], :] * (r_ref[pl.ds(at, 8), :] * keep))
+        for n, o in enumerate(OFFSETS):
+            u_ref[0, rows[n], :] = scaled[n]
+            if o[2] != 1:
+                u_ref[1, rows[n], :] = z_after(scaled[n])
+            if o[2] != -1:
+                u_ref[2, rows[n], :] = z_before(scaled[n])
+        return _
+
+    lax.fori_loop(0, up // 8, scale, 0, unroll=3)
+
+    for who in range(count_ref.shape[0]):
+        count_ref[who] = 0
+
+    def place(x):
+        for y in range(ny):
+            row = slot_ref[x, y]
+            c = x * ny + y
+            for n in range(0, PITCH, 8):
+                size = min(8, PITCH - n)
+                out_ref[pl.ds(row + n, size), :] = s_ref[pl.ds(n * nx * ny + c, size, stride=nx * ny), :]
 
     def galerkin(x, _):
+        for y in range(ny):
+            who = owner_ref[x, y]
+            rank = count_ref[who]
+            count_ref[who] = rank + 1
+            slot_ref[x, y] = (who * 2 + rank) * PITCH
         for yb in range(0, ny, 8):
 
             def u_at(f, o):
                 plane = OFFSETS.index(f)
                 which = {0: 0, 1: 1, -1: 2}[o[2]]
-                row = plane * up + (x + 1 + o[0]) * UP + yb + 1 + o[1]
+                row = plane * up + (x + 2 + o[0]) * YP + yb + o[1]
                 return u_ref[which, pl.ds(row, 8), :]
 
             own = {f: u_at(f, (0, 0, 0)) for f in OFFSETS}
@@ -263,7 +281,7 @@
             for f in OFFSETS:
                 p = parity(f)
                 plane = 8 + p // 2 if f[2] == -1 else p
-                t = t_ref[plane, x + 1 - (f[0] == -1), pl.ds(yb + 1 - (f[1] == -1), 8), :]
+                t = t_ref[pl.ds(plane * tp + (x + 2 - (f[0] == -1)) * YP + yb - (f[1] == -1), 8), :]
                 total = t * own[f]
                 for d in range(3):
                     for step in (-1, 1):
@@ -295,28 +313,7 @@
 
     lax.fori_loop(0, nx, galerkin, 0)
 
-    def clear(i, _):
-        rows = 2 * 2 * PITCH
-        out_ref[pl.ds(pl.multiple_of(i * rows, 8), rows), :] = jnp.zeros((rows, nz), jnp.float32)
-        count_ref[2 * i] = 0
-        count_ref[2 * i + 1] = 0
-        return _
-
-    lax.fori_loop(0, out_ref.shape[0] // (2 * 2 * PITCH), clear, 0)
-
-    def place(x, _):
-        for y in range(ny):
-            who = owner_ref[x, y]
-            rank = count_ref[who]
-            count_ref[who] = rank + 1
-            row = (who * 2 + rank) * PITCH
-            c = x * ny + y
-            for n in (0, 8, 16, 24):
-                size = min(8, PITCH - n)
-                out_ref[pl.ds(row + n, size), :] = s_ref[pl.ds(n * nx * ny + c, size, stride=nx * ny), :]
-        return _
-
-    lax.fori_loop(0, nx, place, 0)
+    lax.fori_loop(0, nx, lambda x, _: (place(x), _)[1], 0)
 
 
 def unpack_kernel(in_ref, out_ref):
@@ -344,6 +341,7 @@
     devices = lax.axis_size("gx") * lax.axis_size("gy")
     k = coefficient.reshape(8, nx, ny, nz)
     ex, ey, hx, hy = nx + 3, ny + 3, nx + 2, ny + 2
+    fine, ratio = (ex + 1) * YP, (nx + 2) * YP
     vmem = pl.BlockSpec(memory_space=pltpu.VMEM)
     smem = pl.BlockSpec(memory_space=pltpu.SMEM)
     f32 = lambda *shape: jax.ShapeDtypeStruct(shape, jnp.float32)
@@ -383,12 +381,14 @@
         functools.partial(main_kernel, nx, ny), "stencils", f32(devices * 2 * PITCH, nz),
         (owner, k, xlo, xhi, ylo, yhi, *layers, inner, side), us=12, first=smem,
         scratch=[
-            pltpu.VMEM((8, ex, YP, nz), jnp.float32),
-            pltpu.VMEM((12, ex, YP, nz), jnp.float32),
+            pltpu.VMEM((8 * fine, nz), jnp.float32),
+            pltpu.VMEM((12 * fine, nz), jnp.float32),
             pltpu.VMEM((ex, 5, 16, nz), jnp.bfloat16),
-            pltpu.VMEM((12, nx + 1, 24, nz), jnp.float32),
-            pltpu.VMEM((3, 27 * hx * UP, nz), jnp.float32),
+            pltpu.VMEM((12 * ratio, nz), jnp.float32),
+            pltpu.VMEM((3, 27 * (hx + 1) * YP, nz), jnp.float32),
+            pltpu.VMEM(((hx + 1) * YP, nz), jnp.float32),
             pltpu.VMEM((PITCH * nx * ny, nz), jnp.float32),
+            pltpu.SMEM((nx, ny), jnp.int32),
             pltpu.SMEM((devices,), jnp.int32),
         ])
     got = lax.all_to_all(out.reshape(devices, -1, 4, nz), ("gx", "gy"), split_axis=0, concat_axis=0, tiled=True)

time: 93.9 us -> 90.7 us (0.966)
  Pallas kernels: 23.8 us -> 20.7 us
    pallas_call x5, Pallas kernels: 21.6 us -> 18.4 us  [call(): pl.pallas_call(kernel, out_shape=out_shape, in_specs=[first] + [vmem] * (...]
  transfers between devices with their start and end apart: 4 -> 4, of which waited for: 0 -> 0; matrix products, arithmetic and copies ran while one was open for 0% -> 0% of each run, Pallas kernels for 11% -> 10%
where the time goes in v4:
time: 90.7 us; the launch traced here: 90.5 us
  blocking collectives  55.5 us (61%)
  Pallas kernels  20.7 us (23%)
  starting transfers between devices  12.8 us (14%)
  local copies, waits for them, and re-layouts  1.23 us (1%)
    all_to_all x1, blocking collectives, per_device(): lax.all_to_all(out.reshape(devices, -1, 4, nz), ('gx', 'gy'), split_axis=...  55.5 us
    pallas_call x5, Pallas kernels, call(): pl.pallas_call(kernel, out_shape=out_shape, in_specs=[first] + [vmem] * (...  18.4 us
    ppermute x4, starting transfers between devices, send(): return lax.ppermute(v, axis, pairs)  12.8 us
    pallas_call x1, Pallas kernels, per_device(): pl.pallas_call(unpack_kernel, grid=(3,), out_shape=f32(27, devices * 2, n...  2.28 us
  transfers between devices with their start and end apart: 4, of which 0 were waited for; matrix products, arithmetic and copies ran while one was open for 0% of the time, Pallas kernels for 10%

profile of v4, /device:TPU:1, one launch (start us, length us, event | category | flops | bytes accessed | tf_op | source)
XLA Modules:
  0.0 90.5 jit_solution(11218947336532994937)
XLA Ops:
  0.0 0.0 copy-start.5
  0.0 0.0 copy-start.6
  0.0 0.0 copy-start
  0.0 1.1 %copy-done = f32[2,2,2,8,16,128]{5,4,3,2,1,0:T(8,128)S(1)} copy-done((f32[2,2,2,8,16,128]{5,4,3,2,1,0:T(8,128)S(1)}, f32[2,2,2,8,16,128]{5,4,3,2,1,0:T(8,128)}, u32[]{:S(2)}) %copy-start) | copy-done | bytes 524312
  1.1 0.0 copy-start.8
  1.1 0.0 copy-start.1
  1.1 0.0 copy-start.2
  1.1 0.0 copy-start.7
  1.1 1.4 %collective-permute-start.1 = (f32[8,1,16,128]{3,2,1,0:T(8,128)S(1)}, f32[8,1,16,128]{3,2,1,0:T(8,128)S(1)}, u32[]{:S(2)}, u32[]{:S(2)}) collective-permute-start(f32[8,1,16,128]{3,2,1,0:T(8,128)S(1)} %get-tuple-element.17), channel_id=1, source_target_pairs={{8,0},{16,8},{24,16},{32,24},{40,32},{48,40},{56,48},{64,56},{72,6... | collective-permute-start | bytes 196616 | tf_op jit(solution)/shard_map/ppermute | solution.py:365
  2.5 4.6 %collective-permute-start = (f32[8,2,16,128]{3,2,1,0:T(8,128)S(1)}, f32[8,2,16,128]{3,2,1,0:T(8,128)S(1)}, u32[]{:S(2)}, u32[]{:S(2)}) collective-permute-start(f32[8,2,16,128]{3,2,1,0:T(8,128)S(1)} %get-tuple-element.16), channel_id=1, source_target_pairs={{0,8},{8,16},{16,24},{24,32},{32,40},{40,48},{48,56},{56,64},{64,7... | collective-permute-start | bytes 393224 | tf_op jit(solution)/shard_map/ppermute | solution.py:365
  7.1 0.0 copy-done.8
  7.1 0.1 copy.9.win_ref
  7.3 0.0 copy-done.5
  7.3 0.0 copy-done.6
  7.3 0.0 copy-done.1
  7.3 0.0 copy-done.2
  7.3 0.0 copy-done.3
  7.3 0.0 copy-done.7
  7.3 6.1 %inner.1 = (bf16[128,64]{1,0:T(8,128)(2,1)S(1)}, f32[128,1]{1,0:T(8,128)S(1)}, bf16[2,128,128]{2,1,0:T(8,128)(2,1)S(1)}, f32[2,128,1]{2,1,0:T(8,128)S(1)}, bf16[...) custom-call(f32[8,8,16,128]{3,2,1,0:T(8,128)S(1)} %bitcast.9, ...), custom_call_target="tpu_custom_call" | custom-call | flops 7000000000 | bytes 1048576 | tf_op jit(solution)/shard_map/inner/pallas_call | solution.py:351
  13.4 0.0 collective-permute-done.1.xhi_ref
  13.4 0.0 collective-permute-done.xlo_ref
  13.5 0.1 send_y.1
  13.5 3.3 %collective-permute-start.3 = (f32[8,11,1,128]{3,2,1,0:T(1,128)S(1)}, f32[8,11,1,128]{3,2,1,0:T(1,128)S(1)}, u32[]{:S(2)}, u32[]{:S(2)}) collective-permute-start(f32[8,11,1,128]{3,2,1,0:T(1,128)S(1)} %get-tuple-element.19), channel_id=1, source_target_pairs={{1,0},{2,1},{3,2},{4,3},{5,4},{6,5},{7,6},{9,8},{10,9},{11,10},{12... | collective-permute-start | bytes 135176 | tf_op jit(solution)/shard_map/ppermute | solution.py:365
  16.8 3.5 %collective-permute-start.2 = (f32[8,11,2,128]{3,2,1,0:T(2,128)S(1)}, f32[8,11,2,128]{3,2,1,0:T(2,128)S(1)}, u32[]{:S(2)}, u32[]{:S(2)}) collective-permute-start(f32[8,11,2,128]{3,2,1,0:T(2,128)S(1)} %get-tuple-element.18), channel_id=1, source_target_pairs={{0,1},{1,2},{2,3},{3,4},{4,5},{5,6},{6,7},{8,9},{9,10},{10,11},{11... | collective-permute-start | bytes 270344 | tf_op jit(solution)/shard_map/ppermute | solution.py:365
  20.4 0.0 copy-start.4
  20.4 3.1 %side.1.side_ref = f32[45,32,128]{2,1,0:T(8,128)S(1)} custom-call(f32[8,8,16,128]{3,2,1,0:T(8,128)S(1)} %bitcast.11, f32[8,2,16,128]{3,2,1,0:T(8,128)S(1)} %collective-permute-done.xlo_ref, f32[8,1,16,128]{3,2,1,0:T(8,128)S(1)} %collective-permute-done.1.xhi_ref, bf16[128,64]{1,0:T(8,128)(2,1)S(1)} %get-tuple-element.20.w1_ref, ...), custom_call_target="tpu_custom_call" | custom-call | flops 4000000000 | bytes 1048576 | tf_op jit(solution)/shard_map/side/pallas_call | solution.py:351
  23.4 0.0 collective-permute-done.3.yhi_ref
  23.5 0.0 collective-permute-done.2.ylo_ref
  23.5 0.0 copy-done.4
  23.5 9.2 %stencils.1 = f32[6656,128]{1,0:T(8,128)S(1)} custom-call(s32[8,16]{1,0:T(8,128)S(1)} %copy-done.4, f32[8,8,16,128]{3,2,1,0:T(8,128)S(1)} %bitcast.12, f32[8,2,16,128]{3,2,1,0:T(8,128)S(1)} %collective-permute-done.xlo_ref, f32[8,1,16,128]{3,2,1,0:T(8,128)S(1)} %collective-permute-done.1.xhi_ref, f32[8,11,2,128]{3,2,1,0:T(2,128)S(1)} %collective-permute-done.2.ylo_ref, ...), custom_call_target="tpu_custom_call" | custom-call | flops 12000000000 | bytes 1048576 | tf_op jit(solution)/shard_map/stencils/pallas_call | solution.py:351
  32.7 55.5 %all_to_all.5 = f32[128,13,4,128]{3,2,1,0:T(4,128)S(1)} all-to-all(f32[128,13,4,128]{3,2,1,0:T(4,128)S(1)} %bitcast.7), channel_id=1, replica_groups=mesh['gx'=16,'gy'=8] {'gx','gy'}, dimensions={0} | all-to-all | bytes 6815744 | tf_op jit(solution)/shard_map/all_to_all | solution.py:394
  88.2 2.3 %unpack.1 = f32[27,256,128]{2,1,0:T(8,128)} custom-call(f32[6656,128]{1,0:T(8,128)S(1)} %bitcast.6), custom_call_target="tpu_custom_call" | custom-call | tf_op jit(solution)/shard_map/unpack/pallas_call | solution.py:395
  (2 shorter events, 0.0 us)
Async XLA Ops:
  0.0 7.3 %copy-start.5 = (f32[2,128]{1,0:T(2,128)S(1)}, f32[2,128]{1,0:T(2,128)}, u32[]{:S(2)}) copy-start(f32[2,128]{1,0:T(2,128)} %bmid_ref.1) | copy-start | bytes 3076
  0.0 7.3 %copy-start.6 = (f32[128]{0:T(128)S(1)}, f32[128]{0:T(128)}, u32[]{:S(2)}) copy-start(f32[128]{0:T(128)} %param.11) | copy-start | bytes 1540
  0.0 1.1 %copy-start = (f32[2,2,2,8,16,128]{5,4,3,2,1,0:T(8,128)S(1)}, f32[2,2,2,8,16,128]{5,4,3,2,1,0:T(8,128)}, u32[]{:S(2)}) copy-start(f32[2,2,2,8,16,128]{5,4,3,2,1,0:T(8,128)} %param.8) | copy-start | bytes 1572868
  1.1 6.1 %copy-start.8 = (bf16[128,27]{0,1:T(8,128)(2,1)S(1)}, bf16[128,27]{0,1:T(8,128)(2,1)}, u32[]{:S(2)}) copy-start(bf16[128,27]{0,1:T(8,128)(2,1)} %param.10) | copy-start | bytes 20740
  1.1 6.2 %copy-start.1 = (f32[2,2,2,8,16,128]{5,4,3,2,1,0:T(8,128)S(1)}, f32[2,2,2,8,16,128]{5,4,3,2,1,0:T(8,128)}, u32[]{:S(2)}) copy-start(f32[2,2,2,8,16,128]{5,4,3,2,1,0:T(8,128)} %param.8) | copy-start | bytes 1572868
  1.1 6.2 %copy-start.2 = (bf16[2,128,128]{2,1,0:T(8,128)(2,1)S(1)}, bf16[2,128,128]{2,1,0:T(8,128)(2,1)}, u32[]{:S(2)}) copy-start(bf16[2,128,128]{2,1,0:T(8,128)(2,1)} %wmid_ref.1) | copy-start | bytes 196612
  1.1 6.2 %copy-start.3 = (bf16[27,128]{1,0:T(8,128)(2,1)S(1)}, bf16[27,128]{1,0:T(8,128)(2,1)}, u32[]{:S(2)}) copy-start(bf16[27,128]{1,0:T(8,128)(2,1)} %wout_ref.1) | copy-start | bytes 20740
  1.1 6.2 %copy-start.7 = (f32[27]{0:T(128)S(1)}, f32[27]{0:T(128)}, u32[]{:S(2)}) copy-start(f32[27]{0:T(128)} %param.15) | copy-start | bytes 328
  1.1 12.3 %collective-permute-start.1 = (f32[8,1,16,128]{3,2,1,0:T(8,128)S(1)}, f32[8,1,16,128]{3,2,1,0:T(8,128)S(1)}, u32[]{:S(2)}, u32[]{:S(2)}) collective-permute-start(f32[8,1,16,128]{3,2,1,0:T(8,128)S(1)} %get-tuple-element.17), channel_id=1, source_target_pairs={{8,0},{16,8},{24,16},{32,24},{40,32},{48,40},{56,48},{64,56},{72,6... | collective-permute-start | bytes 196616 | tf_op jit(solution)/shard_map/ppermute | solution.py:365
  2.5 10.9 %collective-permute-start = (f32[8,2,16,128]{3,2,1,0:T(8,128)S(1)}, f32[8,2,16,128]{3,2,1,0:T(8,128)S(1)}, u32[]{:S(2)}, u32[]{:S(2)}) collective-permute-start(f32[8,2,16,128]{3,2,1,0:T(8,128)S(1)} %get-tuple-element.16), channel_id=1, source_target_pairs={{0,8},{8,16},{16,24},{24,32},{32,40},{40,48},{48,56},{56,64},{64,7... | collective-permute-start | bytes 393224 | tf_op jit(solution)/shard_map/ppermute | solution.py:365
  13.5 9.9 %collective-permute-start.3 = (f32[8,11,1,128]{3,2,1,0:T(1,128)S(1)}, f32[8,11,1,128]{3,2,1,0:T(1,128)S(1)}, u32[]{:S(2)}, u32[]{:S(2)}) collective-permute-start(f32[8,11,1,128]{3,2,1,0:T(1,128)S(1)} %get-tuple-element.19), channel_id=1, source_target_pairs={{1,0},{2,1},{3,2},{4,3},{5,4},{6,5},{7,6},{9,8},{10,9},{11,10},{12... | collective-permute-start | bytes 135176 | tf_op jit(solution)/shard_map/ppermute | solution.py:365
  16.8 6.6 %collective-permute-start.2 = (f32[8,11,2,128]{3,2,1,0:T(2,128)S(1)}, f32[8,11,2,128]{3,2,1,0:T(2,128)S(1)}, u32[]{:S(2)}, u32[]{:S(2)}) collective-permute-start(f32[8,11,2,128]{3,2,1,0:T(2,128)S(1)} %get-tuple-element.18), channel_id=1, source_target_pairs={{0,1},{1,2},{2,3},{3,4},{4,5},{5,6},{6,7},{8,9},{9,10},{10,11},{11... | collective-permute-start | bytes 270344 | tf_op jit(solution)/shard_map/ppermute | solution.py:365
  20.4 3.1 %copy-start.4 = (s32[8,16]{1,0:T(8,128)S(1)}, s32[8,16]{1,0:T(8,128)}, u32[]{:S(2)}) copy-start(s32[8,16]{1,0:T(8,128)} %owner_ref.1) | copy-start | bytes 1540

commit v5 on v4

--- a/solution.py
+++ b/solution.py
@@ -107,7 +107,7 @@
             w_ref[(x - 1) * (ny - 1) + y - 1] = w[:, (y - 1) * nz:y * nz]
         return _
 
-    lax.fori_loop(1, nx, row, 0)
+    lax.fori_loop(1, nx, row, 0, unroll=True)
 
 
 def side_kernel(nx, ny, k_ref, xlo_ref, xhi_ref, w1_ref, b1_ref, wm_ref, bm_ref, wo_ref, bo_ref, w_ref, k5_ref, f_ref):
@@ -124,7 +124,7 @@
             f_ref[x, y] = feature_tile(flat[pl.ds(x * ny + y, 8, stride=5 * ny), :])
         return _
 
-    lax.fori_loop(0, 5, tiles, 0)
+    lax.fori_loop(0, 5, tiles, 0, unroll=True)
 
     def row(i, _):
         x = jnp.where(i == 2, 4, i + 1)
@@ -133,7 +133,7 @@
             w_ref[i * (ny - 1) + y - 1] = w[:, (y - 1) * nz:y * nz]
         return _
 
-    lax.fori_loop(0, 3, row, 0)
+    lax.fori_loop(0, 3, row, 0, unroll=True)
 
 
 def main_kernel(nx, ny, owner_ref, coef_ref, xlo_ref, xhi_ref, ylo_ref, yhi_ref,
@@ -175,7 +175,7 @@
                 r_ref[pl.ds(pl.multiple_of((8 + p // 2) * kp + 8 * i, 8), 8), :] = z_before(v)
         return _
 
-    lax.fori_loop(0, kp // 8, roots, 0, unroll=6)
+    lax.fori_loop(0, kp // 8, roots, 0, unroll=12)
 
     def ratios(i, _):
         def at(px, py, pz, dx, dy):
@@ -195,7 +195,7 @@
                 t_ref[pl.ds(pl.multiple_of((8 + p // 2) * tp + 8 * i, 8), 8), :] = z_before(t)
         return _
 
-    lax.fori_loop(0, tp // 8, ratios, 0, unroll=5)
+    lax.fori_loop(0, tp // 8, ratios, 0, unroll=10)
 
     def put(x, y, wy):
         for n in range(0, 27, 8):
@@ -249,7 +249,7 @@
                 u_ref[2, rows[n], :] = z_before(scaled[n])
         return _
 
-    lax.fori_loop(0, up // 8, scale, 0, unroll=3)
+    lax.fori_loop(0, up // 8, scale, 0, unroll=11)
 
     for who in range(count_ref.shape[0]):
         count_ref[who] = 0
@@ -311,7 +311,7 @@
                 s_ref[pl.ds(n * nx * ny + x * ny + yb, 8), :] = total
         return _
 
-    lax.fori_loop(0, nx, galerkin, 0)
+    lax.fori_loop(0, nx, galerkin, 0, unroll=2)
 
     lax.fori_loop(0, nx, lambda x, _: (place(x), _)[1], 0)
 

time: 90.7 us -> 88 us (0.970)
  Pallas kernels: 20.7 us -> 17.5 us
    pallas_call x5, Pallas kernels: 18.4 us -> 15.2 us  [call(): pl.pallas_call(kernel, out_shape=out_shape, in_specs=[first] + [vmem] * (...]
  transfers between devices with their start and end apart: 4 -> 4, of which waited for: 0 -> 0; matrix products, arithmetic and copies ran while one was open for 0% -> 0% of each run, Pallas kernels for 10% -> 8%
where the time goes in v5:
time: 88 us; the launch traced here: 87.8 us
  blocking collectives  56 us (64%)
  Pallas kernels  17.5 us (20%)
  starting transfers between devices  12.8 us (15%)
  local copies, waits for them, and re-layouts  1.23 us (1%)
    all_to_all x1, blocking collectives, per_device(): lax.all_to_all(out.reshape(devices, -1, 4, nz), ('gx', 'gy'), split_axis=...  56 us
    pallas_call x5, Pallas kernels, call(): pl.pallas_call(kernel, out_shape=out_shape, in_specs=[first] + [vmem] * (...  15.2 us
    ppermute x4, starting transfers between devices, send(): return lax.ppermute(v, axis, pairs)  12.8 us
    pallas_call x1, Pallas kernels, per_device(): pl.pallas_call(unpack_kernel, grid=(3,), out_shape=f32(27, devices * 2, n...  2.28 us
  transfers between devices with their start and end apart: 4, of which 0 were waited for; matrix products, arithmetic and copies ran while one was open for 0% of the time, Pallas kernels for 8%

profile of v5, /device:TPU:1, one launch (start us, length us, event | category | flops | bytes accessed | tf_op | source)
XLA Modules:
  0.0 87.8 jit_solution(18161250906441854011)
XLA Ops:
  0.0 0.0 copy-start.5
  0.0 0.0 copy-start.6
  0.0 0.0 copy-start
  0.0 1.1 %copy-done = f32[2,2,2,8,16,128]{5,4,3,2,1,0:T(8,128)S(1)} copy-done((f32[2,2,2,8,16,128]{5,4,3,2,1,0:T(8,128)S(1)}, f32[2,2,2,8,16,128]{5,4,3,2,1,0:T(8,128)}, u32[]{:S(2)}) %copy-start) | copy-done | bytes 524312
  1.1 0.0 copy-start.8
  1.1 0.0 copy-start.1
  1.1 0.0 copy-start.2
  1.1 0.0 copy-start.7
  1.1 1.4 %collective-permute-start.1 = (f32[8,1,16,128]{3,2,1,0:T(8,128)S(1)}, f32[8,1,16,128]{3,2,1,0:T(8,128)S(1)}, u32[]{:S(2)}, u32[]{:S(2)}) collective-permute-start(f32[8,1,16,128]{3,2,1,0:T(8,128)S(1)} %get-tuple-element.17), channel_id=1, source_target_pairs={{8,0},{16,8},{24,16},{32,24},{40,32},{48,40},{56,48},{64,56},{72,6... | collective-permute-start | bytes 196616 | tf_op jit(solution)/shard_map/ppermute | solution.py:365
  2.5 4.6 %collective-permute-start = (f32[8,2,16,128]{3,2,1,0:T(8,128)S(1)}, f32[8,2,16,128]{3,2,1,0:T(8,128)S(1)}, u32[]{:S(2)}, u32[]{:S(2)}) collective-permute-start(f32[8,2,16,128]{3,2,1,0:T(8,128)S(1)} %get-tuple-element.16), channel_id=1, source_target_pairs={{0,8},{8,16},{16,24},{24,32},{32,40},{40,48},{48,56},{56,64},{64,7... | collective-permute-start | bytes 393224 | tf_op jit(solution)/shard_map/ppermute | solution.py:365
  7.1 0.0 copy-done.8
  7.1 0.1 copy.9.win_ref
  7.3 0.0 copy-done.5
  7.3 0.0 copy-done.6
  7.3 0.0 copy-done.1
  7.3 0.0 copy-done.2
  7.3 0.0 copy-done.3
  7.3 0.0 copy-done.7
  7.3 5.0 %inner.1 = (bf16[128,64]{1,0:T(8,128)(2,1)S(1)}, f32[128,1]{1,0:T(8,128)S(1)}, bf16[2,128,128]{2,1,0:T(8,128)(2,1)S(1)}, f32[2,128,1]{2,1,0:T(8,128)S(1)}, bf16[...) custom-call(f32[8,8,16,128]{3,2,1,0:T(8,128)S(1)} %bitcast.9, ...), custom_call_target="tpu_custom_call" | custom-call | flops 7000000000 | bytes 1048576 | tf_op jit(solution)/shard_map/inner/pallas_call | solution.py:351
  12.4 0.0 collective-permute-done.1.xhi_ref
  12.4 0.0 collective-permute-done.xlo_ref
  12.4 0.1 send_y.1
  12.5 3.3 %collective-permute-start.3 = (f32[8,11,1,128]{3,2,1,0:T(1,128)S(1)}, f32[8,11,1,128]{3,2,1,0:T(1,128)S(1)}, u32[]{:S(2)}, u32[]{:S(2)}) collective-permute-start(f32[8,11,1,128]{3,2,1,0:T(1,128)S(1)} %get-tuple-element.19), channel_id=1, source_target_pairs={{1,0},{2,1},{3,2},{4,3},{5,4},{6,5},{7,6},{9,8},{10,9},{11,10},{12... | collective-permute-start | bytes 135176 | tf_op jit(solution)/shard_map/ppermute | solution.py:365
  15.8 3.5 %collective-permute-start.2 = (f32[8,11,2,128]{3,2,1,0:T(2,128)S(1)}, f32[8,11,2,128]{3,2,1,0:T(2,128)S(1)}, u32[]{:S(2)}, u32[]{:S(2)}) collective-permute-start(f32[8,11,2,128]{3,2,1,0:T(2,128)S(1)} %get-tuple-element.18), channel_id=1, source_target_pairs={{0,1},{1,2},{2,3},{3,4},{4,5},{5,6},{6,7},{8,9},{9,10},{10,11},{11... | collective-permute-start | bytes 270344 | tf_op jit(solution)/shard_map/ppermute | solution.py:365
  19.3 0.0 copy-start.4
  19.3 2.2 %side.1.side_ref = f32[45,32,128]{2,1,0:T(8,128)S(1)} custom-call(f32[8,8,16,128]{3,2,1,0:T(8,128)S(1)} %bitcast.11, f32[8,2,16,128]{3,2,1,0:T(8,128)S(1)} %collective-permute-done.xlo_ref, f32[8,1,16,128]{3,2,1,0:T(8,128)S(1)} %collective-permute-done.1.xhi_ref, bf16[128,64]{1,0:T(8,128)(2,1)S(1)} %get-tuple-element.20.w1_ref, ...), custom_call_target="tpu_custom_call" | custom-call | flops 4000000000 | bytes 1048576 | tf_op jit(solution)/shard_map/side/pallas_call | solution.py:351
  21.5 0.0 collective-permute-done.3.yhi_ref
  21.5 0.0 collective-permute-done.2.ylo_ref
  21.6 0.0 copy-done.4
  21.6 7.9 %stencils.1 = f32[6656,128]{1,0:T(8,128)S(1)} custom-call(s32[8,16]{1,0:T(8,128)S(1)} %copy-done.4, f32[8,8,16,128]{3,2,1,0:T(8,128)S(1)} %bitcast.12, f32[8,2,16,128]{3,2,1,0:T(8,128)S(1)} %collective-permute-done.xlo_ref, f32[8,1,16,128]{3,2,1,0:T(8,128)S(1)} %collective-permute-done.1.xhi_ref, f32[8,11,2,128]{3,2,1,0:T(2,128)S(1)} %collective-permute-done.2.ylo_ref, ...), custom_call_target="tpu_custom_call" | custom-call | flops 12000000000 | bytes 1048576 | tf_op jit(solution)/shard_map/stencils/pallas_call | solution.py:351
  29.4 56.0 %all_to_all.5 = f32[128,13,4,128]{3,2,1,0:T(4,128)S(1)} all-to-all(f32[128,13,4,128]{3,2,1,0:T(4,128)S(1)} %bitcast.7), channel_id=1, replica_groups=mesh['gx'=16,'gy'=8] {'gx','gy'}, dimensions={0} | all-to-all | bytes 6815744 | tf_op jit(solution)/shard_map/all_to_all | solution.py:394
  85.5 2.3 %unpack.1 = f32[27,256,128]{2,1,0:T(8,128)} custom-call(f32[6656,128]{1,0:T(8,128)S(1)} %bitcast.6), custom_call_target="tpu_custom_call" | custom-call | tf_op jit(solution)/shard_map/unpack/pallas_call | solution.py:395
  (2 shorter events, 0.0 us)
Async XLA Ops:
  0.0 7.3 %copy-start.5 = (f32[2,128]{1,0:T(2,128)S(1)}, f32[2,128]{1,0:T(2,128)}, u32[]{:S(2)}) copy-start(f32[2,128]{1,0:T(2,128)} %bmid_ref.1) | copy-start | bytes 3076
  0.0 7.3 %copy-start.6 = (f32[128]{0:T(128)S(1)}, f32[128]{0:T(128)}, u32[]{:S(2)}) copy-start(f32[128]{0:T(128)} %param.11) | copy-start | bytes 1540
  0.0 1.1 %copy-start = (f32[2,2,2,8,16,128]{5,4,3,2,1,0:T(8,128)S(1)}, f32[2,2,2,8,16,128]{5,4,3,2,1,0:T(8,128)}, u32[]{:S(2)}) copy-start(f32[2,2,2,8,16,128]{5,4,3,2,1,0:T(8,128)} %param.8) | copy-start | bytes 1572868
  1.1 6.1 %copy-start.8 = (bf16[128,27]{0,1:T(8,128)(2,1)S(1)}, bf16[128,27]{0,1:T(8,128)(2,1)}, u32[]{:S(2)}) copy-start(bf16[128,27]{0,1:T(8,128)(2,1)} %param.10) | copy-start | bytes 20740
  1.1 6.2 %copy-start.1 = (f32[2,2,2,8,16,128]{5,4,3,2,1,0:T(8,128)S(1)}, f32[2,2,2,8,16,128]{5,4,3,2,1,0:T(8,128)}, u32[]{:S(2)}) copy-start(f32[2,2,2,8,16,128]{5,4,3,2,1,0:T(8,128)} %param.8) | copy-start | bytes 1572868
  1.1 6.2 %copy-start.2 = (bf16[2,128,128]{2,1,0:T(8,128)(2,1)S(1)}, bf16[2,128,128]{2,1,0:T(8,128)(2,1)}, u32[]{:S(2)}) copy-start(bf16[2,128,128]{2,1,0:T(8,128)(2,1)} %wmid_ref.1) | copy-start | bytes 196612
  1.1 6.2 %copy-start.3 = (bf16[27,128]{1,0:T(8,128)(2,1)S(1)}, bf16[27,128]{1,0:T(8,128)(2,1)}, u32[]{:S(2)}) copy-start(bf16[27,128]{1,0:T(8,128)(2,1)} %wout_ref.1) | copy-start | bytes 20740
  1.1 6.2 %copy-start.7 = (f32[27]{0:T(128)S(1)}, f32[27]{0:T(128)}, u32[]{:S(2)}) copy-start(f32[27]{0:T(128)} %param.15) | copy-start | bytes 328
  1.1 11.3 %collective-permute-start.1 = (f32[8,1,16,128]{3,2,1,0:T(8,128)S(1)}, f32[8,1,16,128]{3,2,1,0:T(8,128)S(1)}, u32[]{:S(2)}, u32[]{:S(2)}) collective-permute-start(f32[8,1,16,128]{3,2,1,0:T(8,128)S(1)} %get-tuple-element.17), channel_id=1, source_target_pairs={{8,0},{16,8},{24,16},{32,24},{40,32},{48,40},{56,48},{64,56},{72,6... | collective-permute-start | bytes 196616 | tf_op jit(solution)/shard_map/ppermute | solution.py:365
  2.5 9.8 %collective-permute-start = (f32[8,2,16,128]{3,2,1,0:T(8,128)S(1)}, f32[8,2,16,128]{3,2,1,0:T(8,128)S(1)}, u32[]{:S(2)}, u32[]{:S(2)}) collective-permute-start(f32[8,2,16,128]{3,2,1,0:T(8,128)S(1)} %get-tuple-element.16), channel_id=1, source_target_pairs={{0,8},{8,16},{16,24},{24,32},{32,40},{40,48},{48,56},{56,64},{64,7... | collective-permute-start | bytes 393224 | tf_op jit(solution)/shard_map/ppermute | solution.py:365
  12.5 9.1 %collective-permute-start.3 = (f32[8,11,1,128]{3,2,1,0:T(1,128)S(1)}, f32[8,11,1,128]{3,2,1,0:T(1,128)S(1)}, u32[]{:S(2)}, u32[]{:S(2)}) collective-permute-start(f32[8,11,1,128]{3,2,1,0:T(1,128)S(1)} %get-tuple-element.19), channel_id=1, source_target_pairs={{1,0},{2,1},{3,2},{4,3},{5,4},{6,5},{7,6},{9,8},{10,9},{11,10},{12... | collective-permute-start | bytes 135176 | tf_op jit(solution)/shard_map/ppermute | solution.py:365
  15.8 5.8 %collective-permute-start.2 = (f32[8,11,2,128]{3,2,1,0:T(2,128)S(1)}, f32[8,11,2,128]{3,2,1,0:T(2,128)S(1)}, u32[]{:S(2)}, u32[]{:S(2)}) collective-permute-start(f32[8,11,2,128]{3,2,1,0:T(2,128)S(1)} %get-tuple-element.18), channel_id=1, source_target_pairs={{0,1},{1,2},{2,3},{3,4},{4,5},{5,6},{6,7},{8,9},{9,10},{10,11},{11... | collective-permute-start | bytes 270344 | tf_op jit(solution)/shard_map/ppermute | solution.py:365
  19.3 2.2 %copy-start.4 = (s32[8,16]{1,0:T(8,128)S(1)}, s32[8,16]{1,0:T(8,128)}, u32[]{:S(2)}) copy-start(s32[8,16]{1,0:T(8,128)} %owner_ref.1) | copy-start | bytes 1540

commit v6 on v5

--- a/solution.py
+++ b/solution.py
@@ -311,7 +311,7 @@
                 s_ref[pl.ds(n * nx * ny + x * ny + yb, 8), :] = total
         return _
 
-    lax.fori_loop(0, nx, galerkin, 0, unroll=2)
+    lax.fori_loop(0, nx, galerkin, 0, unroll=4)
 
     lax.fori_loop(0, nx, lambda x, _: (place(x), _)[1], 0)
 
@@ -328,7 +328,7 @@
             out_ref[i, pl.ds(k, 8), :] = in_ref[pl.ds(k * PITCH + n, 8, stride=PITCH), :]
         return _
 
-    lax.fori_loop(0, group, one, 0)
+    lax.fori_loop(0, group, one, 0, unroll=3)
 
     @pl.when(pl.program_id(0) == below // group)
     def _():

time: 88 us -> 87.9 us (level)
  no operation moved by 1% of the time
where the time goes in v6:
time: 87.9 us; the launch traced here: 87.6 us
  blocking collectives  56 us (64%)
  Pallas kernels  17.3 us (20%)
  starting transfers between devices  12.8 us (15%)
  local copies, waits for them, and re-layouts  1.23 us (1%)
    all_to_all x1, blocking collectives, per_device(): lax.all_to_all(out.reshape(devices, -1, 4, nz), ('gx', 'gy'), split_axis=...  56 us
    pallas_call x5, Pallas kernels, call(): pl.pallas_call(kernel, out_shape=out_shape, in_specs=[first] + [vmem] * (...  15.1 us
    ppermute x4, starting transfers between devices, send(): return lax.ppermute(v, axis, pairs)  12.8 us
    pallas_call x1, Pallas kernels, per_device(): pl.pallas_call(unpack_kernel, grid=(3,), out_shape=f32(27, devices * 2, n...  2.22 us
  transfers between devices with their start and end apart: 4, of which 0 were waited for; matrix products, arithmetic and copies ran while one was open for 0% of the time, Pallas kernels for 8%

profile of v6, /device:TPU:1, one launch (start us, length us, event | category | flops | bytes accessed | tf_op | source)
XLA Modules:
  0.0 87.6 jit_solution(9086188078447628683)
XLA Ops:
  0.0 0.0 copy-start.5
  0.0 0.0 copy-start.6
  0.0 0.0 copy-start
  0.0 1.1 %copy-done = f32[2,2,2,8,16,128]{5,4,3,2,1,0:T(8,128)S(1)} copy-done((f32[2,2,2,8,16,128]{5,4,3,2,1,0:T(8,128)S(1)}, f32[2,2,2,8,16,128]{5,4,3,2,1,0:T(8,128)}, u32[]{:S(2)}) %copy-start) | copy-done | bytes 524312
  1.1 0.0 copy-start.8
  1.1 0.0 copy-start.1
  1.1 0.0 copy-start.2
  1.1 0.0 copy-start.7
  1.1 1.4 %collective-permute-start.1 = (f32[8,1,16,128]{3,2,1,0:T(8,128)S(1)}, f32[8,1,16,128]{3,2,1,0:T(8,128)S(1)}, u32[]{:S(2)}, u32[]{:S(2)}) collective-permute-start(f32[8,1,16,128]{3,2,1,0:T(8,128)S(1)} %get-tuple-element.17), channel_id=1, source_target_pairs={{8,0},{16,8},{24,16},{32,24},{40,32},{48,40},{56,48},{64,56},{72,6... | collective-permute-start | bytes 196616 | tf_op jit(solution)/shard_map/ppermute | solution.py:365
  2.5 4.6 %collective-permute-start = (f32[8,2,16,128]{3,2,1,0:T(8,128)S(1)}, f32[8,2,16,128]{3,2,1,0:T(8,128)S(1)}, u32[]{:S(2)}, u32[]{:S(2)}) collective-permute-start(f32[8,2,16,128]{3,2,1,0:T(8,128)S(1)} %get-tuple-element.16), channel_id=1, source_target_pairs={{0,8},{8,16},{16,24},{24,32},{32,40},{40,48},{48,56},{56,64},{64,7... | collective-permute-start | bytes 393224 | tf_op jit(solution)/shard_map/ppermute | solution.py:365
  7.1 0.0 copy-done.8
  7.1 0.1 copy.9.win_ref
  7.3 0.0 copy-done.5
  7.3 0.0 copy-done.6
  7.3 0.0 copy-done.1
  7.3 0.0 copy-done.2
  7.3 0.0 copy-done.3
  7.3 0.0 copy-done.7
  7.3 5.0 %inner.1 = (bf16[128,64]{1,0:T(8,128)(2,1)S(1)}, f32[128,1]{1,0:T(8,128)S(1)}, bf16[2,128,128]{2,1,0:T(8,128)(2,1)S(1)}, f32[2,128,1]{2,1,0:T(8,128)S(1)}, bf16[...) custom-call(f32[8,8,16,128]{3,2,1,0:T(8,128)S(1)} %bitcast.9, ...), custom_call_target="tpu_custom_call" | custom-call | flops 7000000000 | bytes 1048576 | tf_op jit(solution)/shard_map/inner/pallas_call | solution.py:351
  12.4 0.0 collective-permute-done.1.xhi_ref
  12.4 0.0 collective-permute-done.xlo_ref
  12.4 0.1 send_y.1
  12.5 3.3 %collective-permute-start.3 = (f32[8,11,1,128]{3,2,1,0:T(1,128)S(1)}, f32[8,11,1,128]{3,2,1,0:T(1,128)S(1)}, u32[]{:S(2)}, u32[]{:S(2)}) collective-permute-start(f32[8,11,1,128]{3,2,1,0:T(1,128)S(1)} %get-tuple-element.19), channel_id=1, source_target_pairs={{1,0},{2,1},{3,2},{4,3},{5,4},{6,5},{7,6},{9,8},{10,9},{11,10},{12... | collective-permute-start | bytes 135176 | tf_op jit(solution)/shard_map/ppermute | solution.py:365
  15.8 3.5 %collective-permute-start.2 = (f32[8,11,2,128]{3,2,1,0:T(2,128)S(1)}, f32[8,11,2,128]{3,2,1,0:T(2,128)S(1)}, u32[]{:S(2)}, u32[]{:S(2)}) collective-permute-start(f32[8,11,2,128]{3,2,1,0:T(2,128)S(1)} %get-tuple-element.18), channel_id=1, source_target_pairs={{0,1},{1,2},{2,3},{3,4},{4,5},{5,6},{6,7},{8,9},{9,10},{10,11},{11... | collective-permute-start | bytes 270344 | tf_op jit(solution)/shard_map/ppermute | solution.py:365
  19.3 0.0 copy-start.4
  19.3 2.2 %side.1.side_ref = f32[45,32,128]{2,1,0:T(8,128)S(1)} custom-call(f32[8,8,16,128]{3,2,1,0:T(8,128)S(1)} %bitcast.11, f32[8,2,16,128]{3,2,1,0:T(8,128)S(1)} %collective-permute-done.xlo_ref, f32[8,1,16,128]{3,2,1,0:T(8,128)S(1)} %collective-permute-done.1.xhi_ref, bf16[128,64]{1,0:T(8,128)(2,1)S(1)} %get-tuple-element.20.w1_ref, ...), custom_call_target="tpu_custom_call" | custom-call | flops 4000000000 | bytes 1048576 | tf_op jit(solution)/shard_map/side/pallas_call | solution.py:351
  21.5 0.0 collective-permute-done.3.yhi_ref
  21.5 0.0 collective-permute-done.2.ylo_ref
  21.6 0.0 copy-done.4
  21.6 7.8 %stencils.1 = f32[6656,128]{1,0:T(8,128)S(1)} custom-call(s32[8,16]{1,0:T(8,128)S(1)} %copy-done.4, f32[8,8,16,128]{3,2,1,0:T(8,128)S(1)} %bitcast.12, f32[8,2,16,128]{3,2,1,0:T(8,128)S(1)} %collective-permute-done.xlo_ref, f32[8,1,16,128]{3,2,1,0:T(8,128)S(1)} %collective-permute-done.1.xhi_ref, f32[8,11,2,128]{3,2,1,0:T(2,128)S(1)} %collective-permute-done.2.ylo_ref, ...), custom_call_target="tpu_custom_call" | custom-call | flops 12000000000 | bytes 1048576 | tf_op jit(solution)/shard_map/stencils/pallas_call | solution.py:351
  29.4 56.0 %all_to_all.5 = f32[128,13,4,128]{3,2,1,0:T(4,128)S(1)} all-to-all(f32[128,13,4,128]{3,2,1,0:T(4,128)S(1)} %bitcast.7), channel_id=1, replica_groups=mesh['gx'=16,'gy'=8] {'gx','gy'}, dimensions={0} | all-to-all | bytes 6815744 | tf_op jit(solution)/shard_map/all_to_all | solution.py:394
  85.4 2.2 %unpack.1 = f32[27,256,128]{2,1,0:T(8,128)} custom-call(f32[6656,128]{1,0:T(8,128)S(1)} %bitcast.6), custom_call_target="tpu_custom_call" | custom-call | tf_op jit(solution)/shard_map/unpack/pallas_call | solution.py:395
  (2 shorter events, 0.0 us)
Async XLA Ops:
  0.0 7.3 %copy-start.5 = (f32[2,128]{1,0:T(2,128)S(1)}, f32[2,128]{1,0:T(2,128)}, u32[]{:S(2)}) copy-start(f32[2,128]{1,0:T(2,128)} %bmid_ref.1) | copy-start | bytes 3076
  0.0 7.3 %copy-start.6 = (f32[128]{0:T(128)S(1)}, f32[128]{0:T(128)}, u32[]{:S(2)}) copy-start(f32[128]{0:T(128)} %param.11) | copy-start | bytes 1540
  0.0 1.1 %copy-start = (f32[2,2,2,8,16,128]{5,4,3,2,1,0:T(8,128)S(1)}, f32[2,2,2,8,16,128]{5,4,3,2,1,0:T(8,128)}, u32[]{:S(2)}) copy-start(f32[2,2,2,8,16,128]{5,4,3,2,1,0:T(8,128)} %param.8) | copy-start | bytes 1572868
  1.1 6.1 %copy-start.8 = (bf16[128,27]{0,1:T(8,128)(2,1)S(1)}, bf16[128,27]{0,1:T(8,128)(2,1)}, u32[]{:S(2)}) copy-start(bf16[128,27]{0,1:T(8,128)(2,1)} %param.10) | copy-start | bytes 20740
  1.1 6.2 %copy-start.1 = (f32[2,2,2,8,16,128]{5,4,3,2,1,0:T(8,128)S(1)}, f32[2,2,2,8,16,128]{5,4,3,2,1,0:T(8,128)}, u32[]{:S(2)}) copy-start(f32[2,2,2,8,16,128]{5,4,3,2,1,0:T(8,128)} %param.8) | copy-start | bytes 1572868
  1.1 6.2 %copy-start.2 = (bf16[2,128,128]{2,1,0:T(8,128)(2,1)S(1)}, bf16[2,128,128]{2,1,0:T(8,128)(2,1)}, u32[]{:S(2)}) copy-start(bf16[2,128,128]{2,1,0:T(8,128)(2,1)} %wmid_ref.1) | copy-start | bytes 196612
  1.1 6.2 %copy-start.3 = (bf16[27,128]{1,0:T(8,128)(2,1)S(1)}, bf16[27,128]{1,0:T(8,128)(2,1)}, u32[]{:S(2)}) copy-start(bf16[27,128]{1,0:T(8,128)(2,1)} %wout_ref.1) | copy-start | bytes 20740
  1.1 6.2 %copy-start.7 = (f32[27]{0:T(128)S(1)}, f32[27]{0:T(128)}, u32[]{:S(2)}) copy-start(f32[27]{0:T(128)} %param.15) | copy-start | bytes 328
  1.1 11.3 %collective-permute-start.1 = (f32[8,1,16,128]{3,2,1,0:T(8,128)S(1)}, f32[8,1,16,128]{3,2,1,0:T(8,128)S(1)}, u32[]{:S(2)}, u32[]{:S(2)}) collective-permute-start(f32[8,1,16,128]{3,2,1,0:T(8,128)S(1)} %get-tuple-element.17), channel_id=1, source_target_pairs={{8,0},{16,8},{24,16},{32,24},{40,32},{48,40},{56,48},{64,56},{72,6... | collective-permute-start | bytes 196616 | tf_op jit(solution)/shard_map/ppermute | solution.py:365
  2.5 9.8 %collective-permute-start = (f32[8,2,16,128]{3,2,1,0:T(8,128)S(1)}, f32[8,2,16,128]{3,2,1,0:T(8,128)S(1)}, u32[]{:S(2)}, u32[]{:S(2)}) collective-permute-start(f32[8,2,16,128]{3,2,1,0:T(8,128)S(1)} %get-tuple-element.16), channel_id=1, source_target_pairs={{0,8},{8,16},{16,24},{24,32},{32,40},{40,48},{48,56},{56,64},{64,7... | collective-permute-start | bytes 393224 | tf_op jit(solution)/shard_map/ppermute | solution.py:365
  12.5 9.1 %collective-permute-start.3 = (f32[8,11,1,128]{3,2,1,0:T(1,128)S(1)}, f32[8,11,1,128]{3,2,1,0:T(1,128)S(1)}, u32[]{:S(2)}, u32[]{:S(2)}) collective-permute-start(f32[8,11,1,128]{3,2,1,0:T(1,128)S(1)} %get-tuple-element.19), channel_id=1, source_target_pairs={{1,0},{2,1},{3,2},{4,3},{5,4},{6,5},{7,6},{9,8},{10,9},{11,10},{12... | collective-permute-start | bytes 135176 | tf_op jit(solution)/shard_map/ppermute | solution.py:365
  15.8 5.8 %collective-permute-start.2 = (f32[8,11,2,128]{3,2,1,0:T(2,128)S(1)}, f32[8,11,2,128]{3,2,1,0:T(2,128)S(1)}, u32[]{:S(2)}, u32[]{:S(2)}) collective-permute-start(f32[8,11,2,128]{3,2,1,0:T(2,128)S(1)} %get-tuple-element.18), channel_id=1, source_target_pairs={{0,1},{1,2},{2,3},{3,4},{4,5},{5,6},{6,7},{8,9},{9,10},{10,11},{11... | collective-permute-start | bytes 270344 | tf_op jit(solution)/shard_map/ppermute | solution.py:365
  19.3 2.2 %copy-start.4 = (s32[8,16]{1,0:T(8,128)S(1)}, s32[8,16]{1,0:T(8,128)}, u32[]{:S(2)}) copy-start(s32[8,16]{1,0:T(8,128)} %owner_ref.1) | copy-start | bytes 1540
